TPU v7x, 32 devices: a whole 2x2x4 slice. The times are simulated.
32 devices in a mesh: rows: 16 (over z, y, x), heads: 2 (over core).
Axes of the slice: x: 2, y: 2, z: 4, core: 2. Of those that a mesh axis runs over, the one named last changes fastest.
Arguments:
- tokens: bfloat16 [32768, 768], P(('rows', 'heads')), may hold values from -6 to 6
- prompt: bfloat16 [100, 768], replicated, may hold values from -6 to 6
- segment_ids: int32 [32, 1024], P('rows'), may hold values from 0 to 3, as said below
- gain_attn: float32 [768], replicated, may hold values from 0.25 to 1.75
- w_query: bfloat16 [768, 768], P(None, 'heads'), may hold values from -0.09375 to 0.09375
- w_key: bfloat16 [768, 768], P(None, 'heads'), may hold values from -0.09375 to 0.09375
- w_value: bfloat16 [768, 768], P(None, 'heads'), may hold values from -0.21875 to 0.21875
- w_attn_out: bfloat16 [768, 768], P('heads'), may hold values from -1 to 1
- bias_table: bfloat16 [32, 12], P(None, 'heads'), may hold values from -4 to 4
- gain_ff: float32 [768], replicated, may hold values from 0.25 to 1.75
- w_in: bfloat16 [768, 3072], P(None, 'heads'), may hold values from -0.21875 to 0.21875
- w_out: bfloat16 [3072, 768], P('heads'), may hold values from -0.15625 to 0.15625
- out_grad: bfloat16 [32768, 768], P(('rows', 'heads')), may hold values from -6 to 6
Outputs:
- result: bfloat16 [32768, 768], P(('rows', 'heads'))
- grad_tokens: bfloat16 [32768, 768], P(('rows', 'heads'))
- grad_prompt: float32 [100, 768], replicated
- grad_gain_attn: float32 [768], replicated
- grad_w_query: float32 [768, 768], P(None, 'heads')
- grad_w_key: float32 [768, 768], P(None, 'heads')
- grad_w_value: float32 [768, 768], P(None, 'heads')
- grad_w_attn_out: float32 [768, 768], P('heads')
- grad_bias_table: float32 [32, 12], P(None, 'heads')
- grad_gain_ff: float32 [768], replicated
- grad_w_in: float32 [768, 3072], P(None, 'heads')
- grad_w_out: float32 [3072, 768], P('heads')
Inputs may be any that keep to these rules, and one draw needn't show every extreme that they name: `segment_ids`: in each packed row of 1024 tokens the ids run from 0 to 3 in order, never falling; every segment holds 128 tokens or more, and one segment of every row exactly 128.
All inputs are finite; a program needn't handle non-finite values.
Results may differ from a plain program's by a relative error of at most 0.015.
Values may be sent and summed in bfloat16 or wider, within the bound.
A program may use at most 448 MiB of HBM per device.

v0:
```python
from functools import partial
import math

import jax
import jax.numpy as jnp
from jax import lax
from jax.experimental import pallas as pl
from jax.experimental.pallas import tpu as pltpu
from jax.sharding import PartitionSpec as P

D = 768
DH = 64
NB = 32
ROW = 1024
PROMPT = 100
BIG = 1e30
EDGES = (12, 16, 23, 32, 46, 64, 91)
EPS = 1e-06
ROOT_HALF = 1.0 / math.sqrt(2.0)
DENSITY = 1.0 / math.sqrt(2.0 * math.pi)
F32 = jnp.float32
BF16 = jnp.bfloat16
FFC = 128
CH = 768
QB = 256
HOLES = 4
BT = 128
NBLK = ROW // BT


def dot_nn(a, b):
    return lax.dot_general(a, b, (((1,), (0,)), ((), ())), preferred_element_type=F32)


def dot_nt(a, b):
    return lax.dot_general(a, b, (((1,), (1,)), ((), ())), preferred_element_type=F32)


def dot_tn(a, b):
    return lax.dot_general(a, b, (((0,), (0,)), ((), ())), preferred_element_type=F32)


def iota(shape, dim):
    return lax.broadcasted_iota(jnp.int32, shape, dim)


def bucket_of(offset):
    distance = jnp.abs(offset)
    far = jnp.full(distance.shape, 8, jnp.int32)
    for edge in EDGES:
        far = far + (distance >= edge).astype(jnp.int32)
    near = jnp.where(distance < 8, distance, far)
    return near + jnp.where(offset > 0, 16, 0)


def picks_t(seg):
    lane = iota((1, ROW), 1)
    first = jnp.zeros((1, ROW), jnp.int32)
    for s in range(1, 4):
        count = jnp.sum((seg < s).astype(F32), axis=1, keepdims=True).astype(jnp.int32)
        first = jnp.where(seg == s, count, first)
    pos = lane - first
    return (iota((128, ROW), 0) == pos).astype(F32).astype(BF16)


def offset_picks(rows):
    return (bucket_of(256 - iota((rows, 512), 1)) == iota((rows, 512), 0)).astype(F32)


def key_marks(seg):
    i = iota((16, ROW), 0)
    block = iota((16, ROW), 1) // BT
    return jnp.where(i < 8, (seg == i).astype(F32), (block == i - 8).astype(F32)).astype(BF16)


def query_marks(seg, left, right):
    i = iota((16, ROW), 0)
    block = iota((16, ROW), 1) // BT
    excluded = jnp.where(jnp.logical_or(seg == i, i >= 4), 0.0, -BIG)
    j = i - 8
    far = jnp.where(j <= block - 2, left, jnp.where(j >= block + 2, right, 0.0))
    return jnp.where(i < 8, excluded, far).astype(BF16)


def attend_head(h, seg, table_f, qkv_ref, kaug, qaug, near, scores, pt_ref, mixed_ref):
    rows = pl.ds(pl.multiple_of(h * DH, DH), DH)
    values = table_f[pl.ds(h, 1), :]
    near[...] = pltpu.roll(jnp.broadcast_to(values, (BT, 512)), 0, 1, stride=1, stride_axis=0)
    qaug[0:DH, :] = qkv_ref[0, rows, :]
    kaug[0:DH, :] = qkv_ref[1, rows, :]
    qaug[DH : DH + 16, :] = query_marks(seg, values[:, 511:512], values[:, 1:2])
    vt = qkv_ref[2, rows, :]
    ka = kaug[...]
    for b in range(ROW // QB):
        cols = slice(b * QB, (b + 1) * QB)
        sc = scores.at[b % 2]
        sc[...] = dot_tn(ka, qaug[:, cols])
        for u in range(QB // BT):
            qb = b * (QB // BT) + u
            for d in (-1, 0, 1):
                kb = qb + d
                if 0 <= kb < NBLK:
                    sc[kb * BT : (kb + 1) * BT, u * BT : (u + 1) * BT] += near[
                        :, 256 - 128 * d : 384 - 128 * d
                    ]
        s = sc[...]
        peak = jnp.max(s, axis=0, keepdims=True)
        e = jnp.exp(s - peak)
        total = jnp.sum(e, axis=0, keepdims=True)
        p = (e * (1.0 / total)).astype(BF16)
        pt_ref[0, :, cols] = p
        mixed_ref[rows, cols] = dot_nn(vt, p).astype(BF16)


def project_t(w_refs, yt, qkv_ref):
    for m in range(3):
        qkv_ref[m] = dot_tn(w_refs[m][...], yt).astype(BF16)


def head_setup(seg, tab_ref, table_f, kaug):
    picks = offset_picks(NB).astype(BF16)
    table_f[...] = dot_nn(tab_ref[...], picks)
    kaug[DH : DH + 16, :] = key_marks(seg)


def forward_first(
    seg_ref, tok_ref, prompt_ref, gain_ref, wq, wk, wv, tab_ref,
    start_ref, yt_ref, qkv_ref, pt_ref, mixed_ref,
    table_f, kaug, qaug, near, scores,
):
    h = pl.program_id(0)
    seg = seg_ref[...]

    @pl.when(h == 0)
    def _():
        looked = dot_tn(picks_t(seg), prompt_ref[...])
        here = looked[:, D : D + 128] > 0.5
        tok = tok_ref[...].astype(F32)
        start = jnp.concatenate(
            [
                jnp.where(here, looked[:, c : c + 128], tok[:, c : c + 128])
                for c in range(0, D, 128)
            ],
            axis=1,
        )
        start_ref[...] = start.astype(BF16)
        inv = lax.rsqrt(jnp.mean(start * start, axis=1, keepdims=True) + EPS)
        yt = (start * inv * gain_ref[...]).astype(BF16).T
        yt_ref[...] = yt
        project_t((wq, wk, wv), yt, qkv_ref)
        head_setup(seg, tab_ref, table_f, kaug)

    attend_head(h, seg, table_f, qkv_ref, kaug, qaug, near, scores, pt_ref, mixed_ref)


def forward_second(
    seg_ref, start_ref, yt_ref, gain_ref, wq, wk, wv, tab_ref, mixed_own, wo_own, wo_oth,
    qkv_ref, pt_ref, mixed_ref, middle_ref, x_ref, xt_ref,
    table_f, kaug, qaug, near, scores,
):
    h = pl.program_id(0)
    seg = seg_ref[...]

    @pl.when(h == 0)
    def _():
        project_t((wq, wk, wv), yt_ref[...], qkv_ref)
        head_setup(seg, tab_ref, table_f, kaug)

    attend_head(h, seg, table_f, qkv_ref, kaug, qaug, near, scores, pt_ref, mixed_ref)

    @pl.when(h == pl.num_programs(0) - 1)
    def _():
        attn = dot_tn(mixed_own[...], wo_own[...]) + dot_tn(mixed_ref[...], wo_oth[...])
        middle = start_ref[...].astype(F32) + attn
        middle_ref[...] = middle
        inv = lax.rsqrt(jnp.mean(middle * middle, axis=1, keepdims=True) + EPS)
        x = (middle * inv * gain_ref[...]).astype(BF16)
        x_ref[...] = x
        xt_ref[...] = x.T


def plan_flows(n_rows):
    me = lax.axis_index("rows")
    n_bits = n_rows.bit_length() - 1
    bits = [(me // (1 << b)) % 2 for b in range(n_bits)]
    peers = [me + (1 - 2 * bits[b]) * (1 << b) for b in range(n_bits)]
    rest = list(range(3, n_bits))
    orders = [[0, 2, 1] + rest, [1, 2, 0] + rest]
    share = CH // len(orders)
    flows = []
    for f, order in enumerate(orders):
        size, base, slot = share, f * share, 0
        stages, halved = [], []
        for j, b in enumerate(order):
            if j < n_bits - 1 and size % 32 == 0:
                size = size // 2
                keep = pl.multiple_of(base + bits[b] * size, 16)
                give = pl.multiple_of(base + (1 - bits[b]) * size, 16)
                stages.append(("halve", b, give, size, keep, slot))
                halved.append((b, keep, give, size))
                base = keep
            else:
                stages.append(("swap", b, base, size, base, slot))
            slot += size
        for b, keep, give, n in reversed(halved):
            stages.append(("gather", b, keep, n, give, slot))
            slot += n
        flows.append(stages)
    return flows, peers


def ring_rows(n_rows):
    n_bits = n_rows.bit_length() - 1
    size, total = CH // 2, 0
    for j in range(n_bits):
        if j < n_bits - 1 and size % 32 == 0:
            size = size // 2
            total += size
        total += size
    return total


def whole(shape):
    n = len(shape)
    return pl.BlockSpec(shape, lambda *_: (0,) * n, pipeline_mode=pl.Buffered(1))


def whole_out(shape):
    n = len(shape)
    return pl.BlockSpec(shape, lambda *_: (0,) * n)


def sds(shape, dtype):
    return jax.ShapeDtypeStruct(shape, dtype)


def forward_scratch():
    return [
        pltpu.VMEM((8, 512), F32),
        pltpu.VMEM((DH + 16, ROW), BF16),
        pltpu.VMEM((DH + 16, ROW), BF16),
        pltpu.VMEM((BT, 512), F32),
        pltpu.VMEM((2, ROW, QB), F32),
    ]


PARAMS = dict(vmem_limit_bytes=56 * 1024 * 1024)


def run_first(seg, tok, prompt, gain, wq, wk, wv, tab):
    cols = wq.shape[1]
    heads = cols // DH
    return pl.pallas_call(
        forward_first,
        grid=(heads,),
        in_specs=[whole(a.shape) for a in (seg, tok, prompt, gain, wq, wk, wv, tab)],
        out_specs=[
            whole_out((ROW, D)),
            whole_out((D, ROW)),
            whole_out((3, cols, ROW)),
            pl.BlockSpec((1, ROW, ROW), lambda h: (h, 0, 0)),
            whole_out((cols, ROW)),
        ],
        out_shape=[
            sds((ROW, D), BF16),
            sds((D, ROW), BF16),
            sds((3, cols, ROW), BF16),
            sds((heads, ROW, ROW), BF16),
            sds((cols, ROW), BF16),
        ],
        scratch_shapes=forward_scratch(),
        compiler_params=pltpu.CompilerParams(**PARAMS),
        name="attend_own",
    )(seg, tok, prompt, gain, wq, wk, wv, tab)


def run_second(seg, start, yt, gain, wq, wk, wv, tab, mixed_own, wo_own, wo_oth):
    cols = wq.shape[1]
    heads = cols // DH
    ins = (seg, start, yt, gain, wq, wk, wv, tab, mixed_own, wo_own, wo_oth)
    return pl.pallas_call(
        forward_second,
        grid=(heads,),
        in_specs=[whole(a.shape) for a in ins],
        out_specs=[
            whole_out((3, cols, ROW)),
            pl.BlockSpec((1, ROW, ROW), lambda h: (h, 0, 0)),
            whole_out((cols, ROW)),
            whole_out((ROW, D)),
            whole_out((ROW, D)),
            whole_out((D, ROW)),
        ],
        out_shape=[
            sds((3, cols, ROW), BF16),
            sds((heads, ROW, ROW), BF16),
            sds((cols, ROW), BF16),
            sds((ROW, D), F32),
            sds((ROW, D), BF16),
            sds((D, ROW), BF16),
        ],
        scratch_shapes=forward_scratch(),
        compiler_params=pltpu.CompilerParams(**PARAMS),
        name="attend_other",
    )(*ins)


def norm_back(value, gain, grad):
    inv = lax.rsqrt(jnp.mean(value * value, axis=1, keepdims=True) + EPS)
    scaled = grad * gain
    inner = jnp.mean(scaled * value, axis=1, keepdims=True)
    back = inv * scaled - value * (inv * inv * inv * inner)
    return back, jnp.sum(grad * (value * inv), axis=0, keepdims=True)


def backward(
    n_ff, n_heads, n_rows,
    seg_ref, gain_a_ref, gain_f_ref, win_own, win_oth, wout_own, wout_oth, pt_own, pt_oth,
    x_hbm, xt_hbm, og_hbm, mid_hbm, start_hbm, yt_hbm, qkv_own_hbm, qkv_oth_hbm,
    mix_own_hbm, mix_oth_hbm, wq_own_hbm, wk_own_hbm, wv_own_hbm, wq_oth_hbm, wk_oth_hbm,
    wv_oth_hbm, wo_own_hbm, wo_oth_hbm,
    result_ref, gtok_ref, out_in, out_out, out_q, out_k, out_v, out_o, out_small,
    x, xt, og, mid, qkv, mix, gmix, wqkv, wo, feed, gnf, gnat, dst, dqkv, kaug, vaug, doaug,
    tacc, gvec, gains, ptb, g, xsend, xrecv, ring, load_sem, late_sem, pt_sem, out_sem, xs_sem, xr_sem,
    send_sem, recv_sem,
):
    s = pl.program_id(0)
    heads_half = n_heads // 2
    cols = heads_half * DH
    me = lax.axis_index("heads")
    early = [(x_hbm, x), (xt_hbm, xt), (og_hbm, og)]
    later = [
        (mid_hbm, mid),
        (qkv_own_hbm, qkv.at[0]),
        (qkv_oth_hbm, qkv.at[1]),
        (mix_own_hbm, mix.at[0]),
        (mix_oth_hbm, mix.at[1]),
        (wq_own_hbm, wqkv.at[0, 0]),
        (wk_own_hbm, wqkv.at[0, 1]),
        (wv_own_hbm, wqkv.at[0, 2]),
        (wq_oth_hbm, wqkv.at[1, 0]),
        (wk_oth_hbm, wqkv.at[1, 1]),
        (wv_oth_hbm, wqkv.at[1, 2]),
        (wo_own_hbm, wo.at[0]),
        (wo_oth_hbm, wo.at[1]),
    ]
    n_early = len(early)
    loads = [
        pltpu.make_async_copy(a, b, load_sem.at[i]) for i, (a, b) in enumerate(early + later)
    ]
    late = [
        pltpu.make_async_copy(start_hbm, x, late_sem.at[0]),
        pltpu.make_async_copy(yt_hbm, xt, late_sem.at[1]),
    ]

    def pt_start(i):
        hh = 2 * (i // 4) + i % 2
        for o, ref in enumerate((pt_own, pt_oth)):

            @pl.when((i % 4) // 2 == o)
            def _():
                pltpu.make_async_copy(ref.at[hh], ptb.at[i % 2], pt_sem.at[i % 2]).start()

    n_out = cols // 128
    n_chunks = 2 * n_ff + 4 * n_out + 1
    flows, peers = plan_flows(n_rows)
    n_stages = max(len(f) for f in flows)
    core = {"heads": 1 - me}

    def swap(slot):
        return pltpu.make_async_remote_copy(
            src_ref=xsend.at[slot],
            dst_ref=xrecv.at[slot],
            send_sem=xs_sem.at[slot],
            recv_sem=xr_sem.at[slot],
            device_id=core,
            device_id_type=pl.DeviceIdType.MESH,
        )

    def emit(c, slot, own, oth):
        for blocks, ref in ((own, g.at[c]), (oth, xsend.at[slot])):
            for b, block in enumerate(blocks):
                n = block.shape[0]
                ref[b * n : (b + 1) * n, :] = block.astype(BF16)
        swap(slot).start()

    def collect(c, slot):
        swap(slot).wait()
        g[c] = (g[c].astype(F32) + xrecv[slot].astype(F32)).astype(BF16)

    def stage_copy(f, k, c):
        kind, bit, src, n, keep, slot = flows[f][k]
        par = c % 2
        here = g.at[c, pl.ds(src, n), :]
        return pltpu.make_async_remote_copy(
            src_ref=here,
            dst_ref=ring.at[par, f, slot : slot + n, :],
            send_sem=send_sem.at[f, k, par],
            recv_sem=recv_sem.at[f, k, par],
            device_id={"rows": peers[bit]},
            device_id_type=pl.DeviceIdType.MESH,
        )

    def stage_end(f, k, c):
        kind, bit, src, n, keep, slot = flows[f][k]
        stage_copy(f, k, c).wait()
        part = ring[c % 2, f, slot : slot + n, :]
        if kind != "gather":
            part = (g[c, pl.ds(keep, n), :].astype(F32) + part.astype(F32)).astype(BF16)
        g[c, pl.ds(keep, n), :] = part

    def out_wait(par):
        pltpu.make_async_copy(g.at[0], out_in.at[:, 0:128], out_sem.at[par]).wait()

    def out_start(c):
        par = c % 2

        @pl.when(c >= 2)
        def _():
            out_wait(par)

        def wide(ref, col):
            dst = ref.at[:, pl.ds(pl.multiple_of(col * 128, 128), 128)]
            pltpu.make_async_copy(g.at[c], dst, out_sem.at[par]).start()

        def tall(ref, row):
            for b in range(D // 128):
                dst = ref.at[
                    pl.ds(pl.multiple_of(row * 128, 128), 128), b * 128 : (b + 1) * 128
                ]
                src = g.at[c, b * 128 : (b + 1) * 128, :]
                pltpu.make_async_copy(src, dst, out_sem.at[par]).start()

        base = 2 * n_ff + n_out

        @pl.when(jnp.logical_and(c < 2 * n_ff, c % 2 == 0))
        def _():
            wide(out_in, c // 2)

        @pl.when(jnp.logical_and(c < 2 * n_ff, c % 2 == 1))
        def _():
            tall(out_out, c // 2)

        @pl.when(jnp.logical_and(c >= 2 * n_ff, c < base))
        def _():
            tall(out_o, c - 2 * n_ff)

        for m, ref in enumerate((out_q, out_k, out_v)):

            @pl.when(jnp.logical_and(jnp.logical_and(c >= base, c < n_chunks - 1), (c - base) % 3 == m))
            def _():
                wide(ref, (c - base) // 3)

        @pl.when(c == n_chunks - 1)
        def _():
            tall(out_small, 0)

    hole = n_chunks - 4

    def tick(t):
        for k in range(n_stages, -1, -1):
            v = t - k
            c = jnp.where(v >= hole + HOLES, v - HOLES, v)
            valid = jnp.logical_and(c >= 0, c < n_chunks)
            valid = jnp.logical_and(valid, jnp.logical_or(v < hole, v >= hole + HOLES))

            @pl.when(valid)
            def _():
                for f in range(len(flows)):
                    if 0 < k <= len(flows[f]):
                        stage_end(f, k - 1, c)
                    if k < len(flows[f]):
                        stage_copy(f, k, c).start()
                if k == n_stages:
                    out_start(c)

    def lanes(a):
        return [a[:, k : k + 128] for k in range(0, a.shape[1], 128)]

    @pl.when(s == 0)
    def _():
        for copy in loads:
            copy.start()
        barrier = pltpu.get_barrier_semaphore()
        for peer in [{"rows": p} for p in peers] + [core]:
            pl.semaphore_signal(
                barrier, inc=1, device_id=peer, device_id_type=pl.DeviceIdType.MESH
            )
        pl.semaphore_wait(barrier, len(peers) + 1)
        for copy in loads[:n_early]:
            copy.wait()
        feed[...] = jnp.zeros(feed.shape, F32)
        gnf[...] = jnp.zeros(gnf.shape, F32)

    @pl.when(jnp.logical_and(s >= 1, s <= n_ff))
    def _():
        for j in range(2):
            collect(2 * (s - 1) + j, 3 * ((s - 1) % 2) + j)
        tick(s - 1)

    @pl.when(s < n_ff)
    def _():
        wi = jnp.concatenate([win_own[...], win_oth[...]], axis=1)
        wout = jnp.concatenate([wout_own[...], wout_oth[...]], axis=0)
        pre = dot_nn(x[...], wi)
        cdf = 0.5 * (1.0 + lax.erf(pre * ROOT_HALF))
        active = (pre * cdf).astype(BF16)
        slope = cdf + pre * jnp.exp(-0.5 * pre * pre) * DENSITY
        gact = dot_nt(og[...], wout)
        gpre = (gact * slope).astype(BF16)
        feed[...] += dot_nn(active, wout)
        gnf[...] += dot_nt(gpre, wi)
        dwin = dot_nn(xt[...], gpre)
        dwout = dot_tn(active, og[...])
        emit(2 * s, 3 * (s % 2), [dwin[:, :FFC]], [dwin[:, FFC:]])
        emit(2 * s + 1, 3 * (s % 2) + 1, lanes(dwout[:FFC]), lanes(dwout[FFC:]))

    @pl.when(s == n_ff)
    def _():
        for copy in late:
            copy.start()
        pt_start(0)
        for copy in loads[n_early:]:
            copy.wait()
        middle = mid[...]
        result_ref[...] = (middle + feed[...]).astype(BF16)
        back, gain_grad = norm_back(middle, gain_f_ref[...], gnf[...])
        gmid = og[...].astype(F32) + back
        gains[0:1, :] = gain_grad
        mid[...] = gmid
        ga = gmid.astype(BF16)
        dwo = [dot_nn(mix[o], ga) for o in range(2)]
        for j in range(n_out):
            rows = slice(j * 128, (j + 1) * 128)
            emit(2 * n_ff + j, 3 * (n_ff % 2) + j, lanes(dwo[0][rows]), lanes(dwo[1][rows]))
        for o in range(2):
            gmix[o] = dot_nt(wo[o], ga).astype(BF16)
        gnat[...] = jnp.zeros(gnat.shape, F32)
        kaug[DH:, :] = key_marks(seg_ref[...])
        vaug[DH:, :] = (iota((16, ROW), 0) < 3).astype(F32).astype(BF16)
        gvec[...] = jnp.zeros(gvec.shape, F32)
        for copy in late:
            copy.wait()

    i = s - (n_ff + 1)

    def head_back(o, pt_ref):
        hh = 2 * (i // 4) + i % 2
        rows = pl.ds(pl.multiple_of(hh * DH, DH), DH)
        dot_ = gmix[o, rows, :]
        delta = jnp.sum(dot_.astype(F32) * mix[o, rows, :].astype(F32), axis=0, keepdims=True)
        d1 = delta.astype(BF16).astype(F32)
        d2 = (delta - d1).astype(BF16).astype(F32)
        d3 = delta - d1 - d2
        k = iota((16, ROW), 0)
        vaug[0:DH, :] = qkv[o, 2, rows, :]
        kaug[0:DH, :] = qkv[o, 1, rows, :]
        doaug[0:DH, :] = dot_
        doaug[DH:, :] = jnp.where(
            k == 0, -d1, jnp.where(k == 1, -d2, jnp.where(k == 2, -d3, 0.0))
        ).astype(BF16)
        va = vaug[...]
        ka = kaug[...]
        out_rows = pl.ds(pl.multiple_of(o * 128 + (i % 2) * DH, DH), DH)
        tacc[...] = jnp.zeros(tacc.shape, F32)
        left = jnp.zeros((1, QB), F32)
        right = jnp.zeros((1, QB), F32)
        for b in range(ROW // QB):
            qs = slice(b * QB, (b + 1) * QB)
            dp = dot_tn(va, doaug[:, qs])
            ds = pt_ref[:, qs].astype(F32) * dp
            for u in range(QB // BT):
                qb = b * (QB // BT) + u
                for d in (-1, 0, 1):
                    kb = qb + d
                    if 0 <= kb < NBLK:
                        tacc[:, 256 - 128 * d : 384 - 128 * d] += ds[
                            kb * BT : (kb + 1) * BT, u * BT : (u + 1) * BT
                        ]
            dsb = ds.astype(BF16)
            dst[:, qs] = dsb
            r = dot_nn(ka, dsb)
            dqkv[0, out_rows, qs] = r[:DH].astype(BF16)
            sums = r[DH + 8 :]
            j = iota((8, QB), 0)
            block = b * (QB // BT) + iota((8, QB), 1) // BT
            left = left + jnp.sum(jnp.where(j <= block - 2, sums, 0.0), axis=0, keepdims=True)
            right = right + jnp.sum(jnp.where(j >= block + 2, sums, 0.0), axis=0, keepdims=True)
        dqkv[1, out_rows, :] = dot_nt(qkv[o, 0, rows, :], dst[...]).astype(BF16)
        dqkv[2, out_rows, :] = dot_nt(dot_, pt_ref[...]).astype(BF16)
        flip = (iota((BT, BT), 0) + iota((BT, BT), 1) == BT - 1).astype(F32).astype(BF16)
        near = tacc[...]
        high = near.astype(BF16)
        low = (near - high.astype(F32)).astype(BF16)
        turned = dot_nn(flip, high) + dot_nn(flip, low)
        skew = pltpu.roll(turned, 0, 1, stride=1, stride_axis=0)
        vec = pltpu.roll(jnp.sum(skew, axis=0, keepdims=True), 512 - (BT - 1), 1)
        lane = iota((1, 512), 1)
        vec = vec + jnp.where(lane == 511, jnp.sum(left, axis=1, keepdims=True), 0.0)
        vec = vec + jnp.where(lane == 1, jnp.sum(right, axis=1, keepdims=True), 0.0)
        owner = me + o * (1 - 2 * me)
        gvec[pl.ds(owner * heads_half + hh, 1), :] = vec

    in_heads = jnp.logical_and(i >= 0, i < n_heads)

    @pl.when(i == 0)
    def _():
        for j in range(n_out):
            collect(2 * n_ff + j, 3 * (n_ff % 2) + j)

    after_group = jnp.logical_and(jnp.logical_and(i > 0, i <= n_heads), i % 4 == 0)

    @pl.when(after_group)
    def _():
        e = i // 4 - 1
        for m in range(3):
            collect(2 * n_ff + n_out + 3 * e + m, 3 * ((n_ff + 1 + e) % 2) + m)

    @pl.when(in_heads)
    def _():
        tick(n_ff + 2 * i)
        tick(n_ff + 2 * i + 1)

    @pl.when(in_heads)
    def _():
        @pl.when(i + 1 < n_heads)
        def _():
            pt_start(i + 1)

        pltpu.make_async_copy(pt_own.at[0], ptb.at[i % 2], pt_sem.at[i % 2]).wait()
        head_back((i % 4) // 2, ptb.at[i % 2])

    @pl.when(jnp.logical_and(in_heads, i % 4 == 3))
    def _():
        grp = i // 4
        wcols = pl.ds(pl.multiple_of(grp * 128, 128), 128)
        acc = None
        for m in range(3):
            grad = dqkv[m]
            dw = dot_nt(xt[...], grad)
            emit(
                2 * n_ff + n_out + 3 * grp + m, 3 * ((n_ff + 1 + grp) % 2) + m,
                [dw[:, :128]], [dw[:, 128:]],
            )
            w = jnp.concatenate([wqkv[0, m, :, wcols], wqkv[1, m, :, wcols]], axis=1)
            part = dot_nn(w, grad)
            acc = part if acc is None else acc + part
        gnat[...] += acc

    @pl.when(i == n_heads)
    def _():
        seg = seg_ref[...]
        start = x[...].astype(F32)
        back, gain_grad = norm_back(start, gain_a_ref[...], gnat[...].T)
        gstart = mid[...] + back
        picks = picks_t(seg)
        here = dot_tn(picks, (iota((128, 128), 0) < PROMPT).astype(F32).astype(BF16)) > 0.5
        for c in range(0, D, 128):
            gtok_ref[:, c : c + 128] = jnp.where(here, 0.0, gstart[:, c : c + 128]).astype(BF16)
        high = gstart.astype(BF16)
        low = (gstart - high.astype(F32)).astype(BF16)
        gprompt = dot_nn(picks, high) + dot_nn(picks, low)
        opicks = offset_picks(128).astype(BF16)
        gv = gvec[...]
        g1 = gv.astype(BF16)
        g2 = (gv - g1.astype(F32)).astype(BF16)
        gtab = dot_nt(g1, opicks) + dot_nt(g2, opicks)
        row = iota((128, D), 0)
        small = jnp.where(row < PROMPT, gprompt, 0.0)
        small = jnp.where(row == PROMPT, gain_grad, small)
        small = jnp.where(row == PROMPT + 1, gains[0:1, :], small)
        blocks = lanes(small)
        wide = jnp.concatenate([jnp.zeros((104, 128), F32), gtab, jnp.zeros((8, 128), F32)], axis=0)
        blocks[0] = blocks[0] + wide
        last = n_ff + 1 + n_heads // 4
        emit(n_chunks - 1, 3 * (last % 2), blocks, blocks)
        t0 = n_ff + 2 * n_heads

        @pl.loop(t0, t0 + n_chunks - 1 + HOLES - t0)
        def _(t):
            tick(t)

        collect(n_chunks - 1, 3 * (last % 2))

        @pl.loop(n_chunks - 1 + HOLES, n_chunks + HOLES + n_stages)
        def _(t):
            tick(t)

        out_wait(0)
        out_wait(1)


def run_backward(
    n_rows, seg, gain_a, gain_f, win_own, win_oth, wout_own, wout_oth, pt_own, pt_oth, rest
):
    n_ff = win_own.shape[1] // FFC
    n_heads = 2 * pt_own.shape[0]
    cols = n_heads * DH // 2
    n_chunks = 2 * n_ff + 4 * (cols // 128) + 1
    first = n_ff + 1
    n_stages = 2 * (n_rows.bit_length() - 1)

    def ff(s):
        return jnp.minimum(s, n_ff - 1)

    blk_in = pl.BlockSpec((D, FFC), lambda s: (0, ff(s)))
    blk_out = pl.BlockSpec((FFC, D), lambda s: (ff(s), 0))
    anyspec = pl.BlockSpec(memory_space=pl.ANY)
    return pl.pallas_call(
        partial(backward, n_ff, n_heads, n_rows),
        grid=(first + n_heads + 1,),
        in_specs=[
            whole(seg.shape), whole(gain_a.shape), whole(gain_f.shape),
            blk_in, blk_in, blk_out, blk_out,
        ] + [anyspec] * (2 + len(rest)),
        out_specs=[whole((ROW, D)), whole((ROW, D))] + [anyspec] * 7,
        out_shape=[sds((ROW, D), BF16), sds((ROW, D), BF16)] + [
            sds(shape, BF16)
            for shape in (win_own.shape, wout_own.shape)
            + ((D, cols),) * 3 + ((cols, D), (128, D))
        ],
        scratch_shapes=[
            pltpu.VMEM((ROW, D), BF16),
            pltpu.VMEM((D, ROW), BF16),
            pltpu.VMEM((ROW, D), BF16),
            pltpu.VMEM((ROW, D), F32),
            pltpu.VMEM((2, 3, cols, ROW), BF16),
            pltpu.VMEM((2, cols, ROW), BF16),
            pltpu.VMEM((2, cols, ROW), BF16),
            pltpu.VMEM((2, 3, D, cols), BF16),
            pltpu.VMEM((2, cols, D), BF16),
            pltpu.VMEM((ROW, D), F32),
            pltpu.VMEM((ROW, D), F32),
            pltpu.VMEM((D, ROW), F32),
            pltpu.VMEM((ROW, ROW), BF16),
            pltpu.VMEM((3, 256, ROW), BF16),
            pltpu.VMEM((DH + 16, ROW), BF16),
            pltpu.VMEM((DH + 16, ROW), BF16),
            pltpu.VMEM((DH + 16, ROW), BF16),
            pltpu.VMEM((BT, 512), F32),
            pltpu.VMEM((16, 512), F32),
            pltpu.VMEM((8, D), F32),
            pltpu.VMEM((2, ROW, ROW), BF16),
            pltpu.VMEM((n_chunks, CH, 128), BF16),
            pltpu.VMEM((6, CH, 128), BF16),
            pltpu.VMEM((6, CH, 128), BF16),
            pltpu.VMEM((2, 2, ring_rows(n_rows), 128), BF16),
            pltpu.SemaphoreType.DMA((16,)),
            pltpu.SemaphoreType.DMA((2,)),
            pltpu.SemaphoreType.DMA((2,)),
            pltpu.SemaphoreType.DMA((2,)),
            pltpu.SemaphoreType.DMA((6,)),
            pltpu.SemaphoreType.DMA((6,)),
            pltpu.SemaphoreType.DMA((2, n_stages, 2)),
            pltpu.SemaphoreType.DMA((2, n_stages, 2)),
        ],
        compiler_params=pltpu.CompilerParams(
            vmem_limit_bytes=62 * 1024 * 1024, collective_id=0, has_side_effects=True
        ),
        name="backward",
    )(seg, gain_a, gain_f, win_own, win_oth, wout_own, wout_oth, pt_own, pt_oth, *rest)


def on_device(
    tokens, prompt, segment_ids, gain_attn, w_query, w_key, w_value, w_attn_out, bias_table,
    gain_ff, w_in, w_out, out_grad,
):
    me = lax.axis_index("heads")
    seg = lax.dynamic_slice_in_dim(segment_ids, me, 1, 0)
    prompt_ext = jnp.concatenate(
        [jnp.pad(prompt, ((0, 128 - PROMPT), (0, 0))), jnp.ones((128, 128), BF16)], axis=1
    )
    prompt_ext = jnp.where(jnp.arange(128)[:, None] < PROMPT, prompt_ext, 0)
    swap = [(0, 1), (1, 0)]
    heads_half = bias_table.shape[1]
    tab_own = jnp.pad(bias_table.T, ((0, 8 - heads_half), (0, 0)))

    def other(a):
        return lax.ppermute(a, "heads", swap)

    tab_oth, wq_oth, wk_oth, wv_oth = other(tab_own), other(w_query), other(w_key), other(w_value)
    wo_oth, win_oth, wout_oth = other(w_attn_out), other(w_in), other(w_out)
    gain_a, gain_f = gain_attn[None, :], gain_ff[None, :]
    start, yt, qkv_own, pt_own, mix_own = run_first(
        seg, tokens, prompt_ext, gain_a, w_query, w_key, w_value, tab_own
    )
    qkv_oth, pt_oth, mix_oth, middle, x, xt = run_second(
        seg, start, yt, gain_f, wq_oth, wk_oth, wv_oth, tab_oth, mix_own, w_attn_out, wo_oth
    )
    result, gtok, g_in, g_out, g_q, g_k, g_v, g_wo, small = run_backward(
        lax.axis_size("rows"),
        seg, gain_a, gain_f, w_in, win_oth, w_out, wout_oth, pt_own, pt_oth,
        [x, xt, out_grad, middle, start, yt, qkv_own, qkv_oth, mix_own, mix_oth,
         w_query, w_key, w_value, wq_oth, wk_oth, wv_oth, w_attn_out, wo_oth],
    )
    g_in, g_out, g_q, g_k, g_v, g_wo, small = (
        a.astype(F32) for a in (g_in, g_out, g_q, g_k, g_v, g_wo, small)
    )
    gtab = lax.dynamic_slice(small, (104 + me * heads_half, 0), (heads_half, NB)).T
    return (
        result, gtok, small[:PROMPT], small[PROMPT], g_q, g_k, g_v, g_wo, gtab,
        small[PROMPT + 1], g_in, g_out,
    )


def solution(mesh):
    both = P(("rows", "heads"), None)
    cols = P(None, "heads")
    rows = P("heads", None)
    in_specs = (
        both, P(), P("rows", None), P(), cols, cols, cols, rows, cols, P(), cols, rows, both,
    )
    out_specs = (both, both, P(), P(), cols, cols, cols, rows, cols, P(), cols, rows)
    return jax.shard_map(
        on_device, mesh=mesh, in_specs=in_specs, out_specs=out_specs, check_vma=False
    )
```

profile of v0, /device:TPU:0, one launch (start us, length us, event | category | flops | bytes accessed | tf_op | source)
XLA Modules:
  0.0 314.1 jit_solution(13092585495474371684)
XLA Ops:
  1.7 0.7 pad.10.tab_ref
  2.9 2.5 collective-permute-done.5.tab_ref
  5.7 1.5 collective-permute-done.2.wq.wq_oth_hbm
  7.6 1.3 broadcast_in_dim.20.gain_ref.gain_a_ref
  8.9 1.3 broadcast_in_dim.21.gain_ref.gain_f_ref
  10.2 0.6 constant_dynamic-slice_fusion.seg_ref
  10.8 1.7 fusion.1.prompt_ref
  12.5 28.5 %attend_own.1 = (bf16[1024,768]{1,0:T(8,128)(2,1)}, bf16[768,1024]{1,0:T(8,128)(2,1)}, bf16[3,384,1024]{2,1,0:T(8,128)(2,1)}, bf16[6,1024,1024]{2,1,0:T(8,128)(2,1)}, bf16[384,1024]{1,0:T(8,128)(2,1)}) custom-call(s32[1,1024]{1,0:T(1,128)} %constant_dynamic-slice_fusion.seg_ref, bf16[1024,768]{1,0:T(8,128)(2,1)} %tok_ref.1, ...), custom_call_target="tpu_custom_call" | custom-call | tf_op jit(solution)/shard_map/attend_own/pallas_call | solution.py:253
  41.1 0.8 copy-done.5
  42.2 33.2 %attend_other.1 = (bf16[3,384,1024]{2,1,0:T(8,128)(2,1)}, bf16[6,1024,1024]{2,1,0:T(8,128)(2,1)}, bf16[384,1024]{1,0:T(8,128)(2,1)}, f32[1024,768]{1,0:T(8,128)}...) custom-call(s32[1,1024]{1,0:T(1,128)} %constant_dynamic-slice_fusion.seg_ref, ...), custom_call_target="tpu_custom_call" | custom-call | tf_op jit(solution)/shard_map/attend_other/pallas_call | solution.py:281
  75.4 221.8 %backward.1 = (bf16[1024,768]{1,0:T(8,128)(2,1)}, bf16[1024,768]{1,0:T(8,128)(2,1)}, bf16[768,1536]{1,0:T(8,128)(2,1)}, bf16[1536,768]{1,0:T(8,128)(2,1)}, bf16[...) custom-call(s32[1,1024]{1,0:T(1,128)} %constant_dynamic-slice_fusion, ...), custom_call_target="tpu_custom_call" | custom-call | tf_op jit(solution)/shard_map/backward/pallas_call | solution.py:708
  297.2 1.8 slice.12
  299.0 1.0 convert_element_type.27
  300.0 0.6 slice_reduce_fusion
  300.6 0.6 dynamic-slice_bitcast_fusion
  301.2 1.1 convert_element_type.28
  302.3 1.1 convert_element_type.29
  303.4 1.1 convert_element_type.30
  304.5 1.1 convert_element_type.31
  305.6 2.8 convert_element_type.32
  308.4 2.5 convert_element_type.33
  310.9 1.1 copy.27
  312.1 0.8 copy-done.8
  312.9 1.1 copy.28
  (43 shorter events, 2.8 us)
Async XLA Ops:
  0.6 9.5 %copy-start = (s32[2,1024]{1,0:T(2,128)S(1)}, s32[2,1024]{1,0:T(2,128)}, u32[]{:S(2)}) copy-start(s32[2,1024]{1,0:T(2,128)} %param.15) | copy-start | bytes 24580
  0.7 74.7 %collective-permute-start = (bf16[768,1536]{1,0:T(8,128)(2,1)}, bf16[768,1536]{1,0:T(8,128)(2,1)}, u32[]{:S(2)}, u32[]{:S(2)}) collective-permute-start(bf16[768,1536]{1,0:T(8,128)(2,1)} %win_own.1), channel_id=1, source_target_pairs={{0,1},{1,0},{2,3},{3,2},{4,5},{5,4},{6,7},{7,6},{8,9},{9,8},{10,11... | collective-permute-start | bytes 7077896 | tf_op jit(solution)/shard_map/ppermute | solution.py:778
  1.2 74.2 %collective-permute-start.1 = (bf16[1536,768]{1,0:T(8,128)(2,1)}, bf16[1536,768]{1,0:T(8,128)(2,1)}, u32[]{:S(2)}, u32[]{:S(2)}) collective-permute-start(bf16[1536,768]{1,0:T(8,128)(2,1)} %wout_own.1), channel_id=1, source_target_pairs={{0,1},{1,0},{2,3},{3,2},{4,5},{5,4},{6,7},{7,6},{8,9},{9,8},{10,11... | collective-permute-start | bytes 7077896 | tf_op jit(solution)/shard_map/ppermute | solution.py:778
  1.3 6.0 %collective-permute-start.2 = (bf16[768,384]{1,0:T(8,128)(2,1)}, bf16[768,384]{1,0:T(8,128)(2,1)S(1)}, u32[]{:S(2)}, u32[]{:S(2)}) collective-permute-start(bf16[768,384]{1,0:T(8,128)(2,1)} %wq_own_hbm.1), channel_id=1, source_target_pairs={{0,1},{1,0},{2,3},{3,2},{4,5},{5,4},{6,7},{7,6},{8,9},{9,8},{10,11... | collective-permute-start | bytes 1769480 | tf_op jit(solution)/shard_map/ppermute | solution.py:778
  2.4 10.1 %copy-start.14 = (bf16[8,32]{1,0:T(8,128)(2,1)}, bf16[8,32]{1,0:T(8,128)(2,1)S(1)}, u32[]{:S(2)}) copy-start(bf16[8,32]{1,0:T(8,128)(2,1)S(1)} %pad.10.tab_ref) | copy-start | bytes 1540
  2.4 3.0 collective-permute-start.5
  2.5 38.5 %collective-permute-start.3 = (bf16[768,384]{1,0:T(8,128)(2,1)}, bf16[768,384]{1,0:T(8,128)(2,1)S(1)}, u32[]{:S(2)}, u32[]{:S(2)}) collective-permute-start(bf16[768,384]{1,0:T(8,128)(2,1)} %wk_own_hbm.1), channel_id=1, source_target_pairs={{0,1},{1,0},{2,3},{3,2},{4,5},{5,4},{6,7},{7,6},{8,9},{9,8},{10,11... | collective-permute-start | bytes 1769480 | tf_op jit(solution)/shard_map/ppermute | solution.py:778
  5.3 35.6 %copy-start.15 = (bf16[8,32]{1,0:T(8,128)(2,1)}, bf16[8,32]{1,0:T(8,128)(2,1)S(1)}, u32[]{:S(2)}) copy-start(bf16[8,32]{1,0:T(8,128)(2,1)S(1)} %collective-permute-done.5.tab_ref) | copy-start | bytes 1540
  5.3 35.7 %collective-permute-start.4 = (bf16[768,384]{1,0:T(8,128)(2,1)}, bf16[768,384]{1,0:T(8,128)(2,1)S(1)}, u32[]{:S(2)}, u32[]{:S(2)}) collective-permute-start(bf16[768,384]{1,0:T(8,128)(2,1)} %wv_own_hbm.1), channel_id=1, source_target_pairs={{0,1},{1,0},{2,3},{3,2},{4,5},{5,4},{6,7},{7,6},{8,9},{9,8},{10,11... | collective-permute-start | bytes 1769480 | tf_op jit(solution)/shard_map/ppermute | solution.py:778
  7.2 33.7 %copy-start.4 = (bf16[768,384]{1,0:T(8,128)(2,1)}, bf16[768,384]{1,0:T(8,128)(2,1)S(1)}, u32[]{:S(2)}) copy-start(bf16[768,384]{1,0:T(8,128)(2,1)S(1)} %collective-permute-done.2.wq.wq_oth_hbm) | copy-start | bytes 1769476
  7.2 33.8 %collective-permute-start.6 = (bf16[384,768]{1,0:T(8,128)(2,1)}, bf16[384,768]{1,0:T(8,128)(2,1)S(1)}, u32[]{:S(2)}, u32[]{:S(2)}) collective-permute-start(bf16[384,768]{1,0:T(8,128)(2,1)} %wo_own_hbm.1), channel_id=1, source_target_pairs={{0,1},{1,0},{2,3},{3,2},{4,5},{5,4},{6,7},{7,6},{8,9},{9,8},{10,11... | collective-permute-start | bytes 1769480 | tf_op jit(solution)/shard_map/ppermute | solution.py:778
  41.0 0.8 copy-start.5
  41.0 1.0 copy-start.6
  41.0 1.2 copy-start.7
  297.2 3.9 %copy-start.13 = (bf16[768,384]{1,0:T(8,128)(2,1)S(1)}, bf16[768,384]{1,0:T(8,128)(2,1)}, u32[]{:S(2)}) copy-start(bf16[768,384]{1,0:T(8,128)(2,1)} %get-tuple-element.46) | copy-start | bytes 1769476
  297.2 5.0 %copy-start.12 = (bf16[768,384]{1,0:T(8,128)(2,1)S(1)}, bf16[768,384]{1,0:T(8,128)(2,1)}, u32[]{:S(2)}) copy-start(bf16[768,384]{1,0:T(8,128)(2,1)} %get-tuple-element.47) | copy-start | bytes 1769476
  301.2 2.2 copy-start.11
  302.3 2.2 copy-start.10
  303.4 2.2 copy-start.3
  305.6 2.8 copy-start.2
  308.4 2.5 copy-start.9
  310.9 2.0 copy-start.8
  310.9 3.1 copy-start.1
where the time goes:
time: 314 us
  Pallas kernels  284 us (90%)
  other arithmetic  12.4 us (4%)
  local copies, waits for them, and re-layouts  11.1 us (4%)
  waiting for transfers between devices  3.99 us (1%)
    pallas_call x1, Pallas kernels, run_backward(): pl.pallas_call(partial(backward, n_ff, n_heads, n_rows), grid=(first + n_...  222 us
    pallas_call x1, Pallas kernels, run_second(): pl.pallas_call(forward_second, grid=(heads,), in_specs=[whole(a.shape) fo...  33.2 us
    pallas_call x1, Pallas kernels, run_first(): pl.pallas_call(forward_first, grid=(heads,), in_specs=[whole(a.shape) for...  28.5 us
    convert_element_type x7, other arithmetic, on_device(): a.astype(F32)  10.7 us
  transfers between devices with their start and end apart: 7, of which 2 were waited for; matrix products, arithmetic and copies ran while one was open for 2% of the time, Pallas kernels for 20%

commit v1 on v0

v1 whole, which is shorter than its diff:
```python
from functools import partial
import math

import jax
import jax.numpy as jnp
from jax import lax
from jax.experimental import pallas as pl
from jax.experimental.pallas import tpu as pltpu
from jax.sharding import PartitionSpec as P

D = 768
DH = 64
NB = 32
ROW = 1024
PROMPT = 100
BIG = 1e30
EDGES = (12, 16, 23, 32, 46, 64, 91)
EPS = 1e-06
ROOT_HALF = 1.0 / math.sqrt(2.0)
DENSITY = 1.0 / math.sqrt(2.0 * math.pi)
F32 = jnp.float32
BF16 = jnp.bfloat16
FFC = 128
CH = 768
UNIT = CH
QB = 256
GROUP = 3
SIZES = (2, 3, 4, 5, 6, 8)
SPACING = 3
SLOTS = 7
BT = 128
NBLK = ROW // BT


def dot_nn(a, b):
    return lax.dot_general(a, b, (((1,), (0,)), ((), ())), preferred_element_type=F32)


def dot_nt(a, b):
    return lax.dot_general(a, b, (((1,), (1,)), ((), ())), preferred_element_type=F32)


def dot_tn(a, b):
    return lax.dot_general(a, b, (((0,), (0,)), ((), ())), preferred_element_type=F32)


def own_row(seg_ref):
    return jnp.where(lax.axis_index("heads") == 0, seg_ref[0:1, :], seg_ref[1:2, :])


def iota(shape, dim):
    return lax.broadcasted_iota(jnp.int32, shape, dim)


def bucket_of(offset):
    distance = jnp.abs(offset)
    far = jnp.full(distance.shape, 8, jnp.int32)
    for edge in EDGES:
        far = far + (distance >= edge).astype(jnp.int32)
    near = jnp.where(distance < 8, distance, far)
    return near + jnp.where(offset > 0, 16, 0)


def picks_t(seg):
    lane = iota((1, ROW), 1)
    first = jnp.zeros((1, ROW), jnp.int32)
    for s in range(1, 4):
        count = jnp.sum((seg < s).astype(F32), axis=1, keepdims=True).astype(jnp.int32)
        first = jnp.where(seg == s, count, first)
    pos = lane - first
    return (iota((128, ROW), 0) == pos).astype(F32).astype(BF16)


def offset_picks(rows):
    return (bucket_of(256 - iota((rows, 512), 1)) == iota((rows, 512), 0)).astype(F32)


def key_marks(seg):
    i = iota((16, ROW), 0)
    block = iota((16, ROW), 1) // BT
    return jnp.where(i < 8, (seg == i).astype(F32), (block == i - 8).astype(F32)).astype(BF16)


def query_marks(seg, left, right):
    i = iota((16, ROW), 0)
    block = iota((16, ROW), 1) // BT
    excluded = jnp.where(jnp.logical_or(seg == i, i >= 4), 0.0, -BIG)
    j = i - 8
    far = jnp.where(j <= block - 2, left, jnp.where(j >= block + 2, right, 0.0))
    return jnp.where(i < 8, excluded, far).astype(BF16)


def attend_block(n, q, lo, base, kn, qaug, vaug, strip, pt_ref, mixed_ref, inv_ref):
    lo = jnp.minimum(lo, NBLK - n)
    rows = pl.ds(pl.multiple_of(lo * BT, BT), n * BT)
    cols = pl.ds(pl.multiple_of(q * QB, QB), QB)
    near = pl.ds(pl.multiple_of((lo - q * (QB // BT) + ROW // BT - QB // BT) * BT, BT), n * BT)

    def mix(j):
        o = dot_nn(vaug[j, :, rows], pt_ref[j, rows, :])
        inv = 1.0 / o[DH : DH + 1]
        out = pl.ds(pl.multiple_of((base + j) * DH, DH), DH)
        mixed_ref[out, cols] = (o[:DH] * inv).astype(BF16)
        inv_ref[pl.ds(base + j, 1), cols] = inv

    scores, peaks = [], []
    for j in range(GROUP):
        s = dot_nn(kn[j, rows, :], qaug[j, :, cols]) + strip[j, near, :]
        scores.append(s)
        peaks.append(jnp.max(s, axis=0, keepdims=True))
    for j in range(GROUP):
        if n < NBLK:
            pt_ref[j] = jnp.zeros((ROW, QB), BF16)
        pt_ref[j, rows, :] = jnp.exp(scores[j] - peaks[j]).astype(BF16)
        if j:
            mix(j - 1)
    mix(GROUP - 1)


def attend_heads(
    step, q, seg, table_f, span, qkv_ref, kaug, qaug, vaug, kn, strip, pt_ref, mixed_ref, inv_ref
):
    base = step * GROUP
    per = QB // BT
    zero = (ROW // BT - per) * BT
    @pl.when(q == 0)
    def _():
        for j in range(GROUP):
            rows = pl.ds(pl.multiple_of((base + j) * DH, DH), DH)
            values = table_f[pl.ds(base + j, 1), :]
            near = pltpu.roll(jnp.broadcast_to(values, (BT, 512)), 0, 1, stride=1, stride_axis=0)
            for d in range(-1, per + 1):
                for u in range(per):
                    if abs(d - u) <= 1:
                        at = 256 - 128 * (d - u)
                        strip[j, zero + d * BT : zero + (d + 1) * BT, u * BT : (u + 1) * BT] = near[
                            :, at : at + 128
                        ]
            qaug[j, 0:DH, :] = qkv_ref[0, rows, :]
            kaug[0:DH, :] = qkv_ref[1, rows, :]
            vaug[j, 0:DH, :] = qkv_ref[2, rows, :]
            qaug[j, DH : DH + 16, :] = query_marks(seg, values[:, 511:512], values[:, 1:2])
            kn[j] = kaug[...].T

    lo, n = span[0, q], span[1, q]
    last = 0
    for size in SIZES:

        @pl.when(jnp.logical_and(n > last, n <= size))
        def _():
            attend_block(size, q, lo, base, kn, qaug, vaug, strip, pt_ref, mixed_ref, inv_ref)

        last = size


def project_t(w_refs, yt, qkv_ref):
    for m in range(3):
        qkv_ref[m] = dot_tn(w_refs[m][...], yt).astype(BF16)


def head_setup(seg, tab_ref, table_f, span, kaug, qaug, vaug, strip):
    picks = offset_picks(NB).astype(BF16)
    wide_tab = jnp.concatenate([tab_ref[...], jnp.zeros((NB, 128 - tab_ref.shape[1]), BF16)], axis=1)
    table_f[...] = dot_tn(wide_tab, picks)[0:8]
    kaug[DH:, :] = jnp.zeros((128 - DH, ROW), BF16)
    qaug[:, DH:, :] = jnp.zeros((GROUP, 128 - DH, ROW), BF16)
    kaug[DH : DH + 16, :] = key_marks(seg)
    vaug[:, DH:, :] = jnp.ones((GROUP, 16, ROW), BF16)
    strip[...] = jnp.zeros(strip.shape, F32)
    for q in range(ROW // QB):
        lowest = jnp.min(seg[:, q * QB : (q + 1) * QB].astype(F32))
        highest = jnp.max(seg[:, q * QB : (q + 1) * QB].astype(F32))
        wide = seg.astype(F32)
        begin = jnp.sum((wide < lowest).astype(F32)).astype(jnp.int32) // BT
        end = (jnp.sum((wide <= highest).astype(F32)).astype(jnp.int32) + BT - 1) // BT
        span[0, q] = begin
        span[1, q] = end - begin


def forward_first(
    seg_ref, tok_ref, prompt_ref, gain_ref, wq, wk, wv, tab_ref,
    start_ref, yt_ref, qkv_ref, pt_ref, mixed_ref, inv_ref,
    table_f, span, kaug, qaug, vaug, kn, strip, padded,
):
    step, q = pl.program_id(0), pl.program_id(1)
    first = jnp.logical_and(step == 0, q == 0)
    seg = own_row(seg_ref)

    @pl.when(first)
    def _():
        padded[...] = jnp.zeros(padded.shape, BF16)
        padded[0:PROMPT, :] = prompt_ref[...]
        picks = picks_t(seg)
        looked = dot_tn(picks, padded[...])
        here = dot_tn(picks, (iota((128, 128), 0) < PROMPT).astype(F32).astype(BF16)) > 0.5
        tok = tok_ref[...].astype(F32)
        start = jnp.concatenate(
            [
                jnp.where(here, looked[:, c : c + 128], tok[:, c : c + 128])
                for c in range(0, D, 128)
            ],
            axis=1,
        )
        start_ref[...] = start.astype(BF16)
        inv = lax.rsqrt(jnp.mean(start * start, axis=1, keepdims=True) + EPS)
        yt = (start * inv * gain_ref[...][None, :]).astype(BF16).T
        yt_ref[...] = yt
        project_t((wq, wk, wv), yt, qkv_ref)
        head_setup(seg, tab_ref, table_f, span, kaug, qaug, vaug, strip)

    attend_heads(
        step, q, seg, table_f, span, qkv_ref, kaug, qaug, vaug, kn, strip, pt_ref, mixed_ref, inv_ref
    )


def forward_second(
    seg_ref, start_ref, yt_ref, gain_ref, wq, wk, wv, tab_ref, mixed_own, wo_own, wo_oth,
    qkv_ref, pt_ref, mixed_ref, inv_ref, middle_ref, x_ref, xt_ref,
    table_f, span, kaug, qaug, vaug, kn, strip,
):
    step, q = pl.program_id(0), pl.program_id(1)
    first = jnp.logical_and(step == 0, q == 0)
    seg = own_row(seg_ref)

    @pl.when(first)
    def _():
        project_t((wq, wk, wv), yt_ref[...], qkv_ref)
        head_setup(seg, tab_ref, table_f, span, kaug, qaug, vaug, strip)

    attend_heads(
        step, q, seg, table_f, span, qkv_ref, kaug, qaug, vaug, kn, strip, pt_ref, mixed_ref, inv_ref
    )

    @pl.when(jnp.logical_and(step == pl.num_programs(0) - 1, q == pl.num_programs(1) - 1))
    def _():
        attn = dot_tn(mixed_own[...], wo_own[...]) + dot_tn(mixed_ref[...], wo_oth[...])
        middle = start_ref[...].astype(F32) + attn
        middle_ref[...] = middle
        inv = lax.rsqrt(jnp.mean(middle * middle, axis=1, keepdims=True) + EPS)
        x = (middle * inv * gain_ref[...][None, :]).astype(BF16)
        x_ref[...] = x
        xt_ref[...] = x.T


def plan_stages(n_rows):
    n_bits = n_rows.bit_length() - 1
    size, slot = UNIT, 0
    stages, halved = [], []
    for j in range(n_bits):
        if j < n_bits - 1 and size % 32 == 0:
            size = size // 2
            halved.append((j, size))
            stages.append(("halve", j, size, slot))
        else:
            stages.append(("swap", j, size, slot))
        slot += size
    for j, n in reversed(halved):
        stages.append(("gather", j, n, slot))
        slot += n
    return stages, len(halved), slot


def stage_order(n_rows, odd):
    n_bits = n_rows.bit_length() - 1
    me = lax.axis_index("rows")
    bits = [(me // (1 << b)) % 2 for b in range(n_bits)]
    peers = [me + (1 - 2 * bits[b]) * (1 << b) for b in range(n_bits)]
    even = [0, 2, 1] + list(range(3, n_bits))
    flip = [1, 2, 0] + list(range(3, n_bits))
    pick = [(bits[a] + odd * (bits[b] - bits[a])) for a, b in zip(even, flip)]
    peer = [(peers[a] + odd * (peers[b] - peers[a])) for a, b in zip(even, flip)]
    return pick, peer, peers


def whole(shape):
    n = len(shape)
    return pl.BlockSpec(shape, lambda *_: (0,) * n, pipeline_mode=pl.Buffered(1))


def whole_out(shape):
    n = len(shape)
    return pl.BlockSpec(shape, lambda *_: (0,) * n)


def sds(shape, dtype):
    return jax.ShapeDtypeStruct(shape, dtype)


def forward_scratch():
    return [
        pltpu.VMEM((8, 512), F32),
        pltpu.SMEM((2, ROW // QB), jnp.int32),
        pltpu.VMEM((128, ROW), BF16),
        pltpu.VMEM((GROUP, 128, ROW), BF16),
        pltpu.VMEM((GROUP, DH + 16, ROW), BF16),
        pltpu.VMEM((GROUP, ROW, 128), BF16),
        pltpu.VMEM((GROUP, 2 * ROW, QB), F32),
    ]


PARAMS = dict(vmem_limit_bytes=56 * 1024 * 1024)


def run_first(seg, tok, prompt, gain, wq, wk, wv, tab):
    cols = wq.shape[1]
    heads = cols // DH
    return pl.pallas_call(
        forward_first,
        grid=(heads // GROUP, ROW // QB),
        in_specs=[whole(a.shape) for a in (seg, tok, prompt, gain, wq, wk, wv, tab)],
        out_specs=[
            whole_out((ROW, D)),
            whole_out((D, ROW)),
            whole_out((3, cols, ROW)),
            pl.BlockSpec((GROUP, ROW, QB), lambda h, q: (h, 0, q)),
            whole_out((cols, ROW)),
            whole_out((8, ROW)),
        ],
        out_shape=[
            sds((ROW, D), BF16),
            sds((D, ROW), BF16),
            sds((3, cols, ROW), BF16),
            sds((heads, ROW, ROW), BF16),
            sds((cols, ROW), BF16),
            sds((8, ROW), F32),
        ],
        scratch_shapes=forward_scratch() + [pltpu.VMEM((128, D), BF16)],
        compiler_params=pltpu.CompilerParams(**PARAMS),
        cost_estimate=pl.CostEstimate(flops=2 * 10**10, bytes_accessed=10**7, transcendentals=0),
        name="attend_own",
    )(seg, tok, prompt, gain, wq, wk, wv, tab)


def run_second(seg, start, yt, gain, wq, wk, wv, tab, mixed_own, wo_own, wo_oth):
    cols = wq.shape[1]
    heads = cols // DH
    ins = (seg, start, yt, gain, wq, wk, wv, tab, mixed_own, wo_own, wo_oth)
    return pl.pallas_call(
        forward_second,
        grid=(heads // GROUP, ROW // QB),
        in_specs=[whole(a.shape) for a in ins],
        out_specs=[
            whole_out((3, cols, ROW)),
            pl.BlockSpec((GROUP, ROW, QB), lambda h, q: (h, 0, q)),
            whole_out((cols, ROW)),
            whole_out((8, ROW)),
            whole_out((ROW, D)),
            whole_out((ROW, D)),
            whole_out((D, ROW)),
        ],
        out_shape=[
            sds((3, cols, ROW), BF16),
            sds((heads, ROW, ROW), BF16),
            sds((cols, ROW), BF16),
            sds((8, ROW), F32),
            sds((ROW, D), F32),
            sds((ROW, D), BF16),
            sds((D, ROW), BF16),
        ],
        scratch_shapes=forward_scratch(),
        compiler_params=pltpu.CompilerParams(**PARAMS),
        cost_estimate=pl.CostEstimate(flops=2 * 10**10, bytes_accessed=10**7, transcendentals=0),
        name="attend_other",
    )(*ins)


def norm_back(value, gain, grad):
    inv = lax.rsqrt(jnp.mean(value * value, axis=1, keepdims=True) + EPS)
    scaled = grad * gain
    inner = jnp.mean(scaled * value, axis=1, keepdims=True)
    back = inv * scaled - value * (inv * inv * inv * inner)
    return back, jnp.sum(grad * (value * inv), axis=0, keepdims=True)


def backward(
    n_ff, n_heads, n_rows,
    seg_ref, gain_a_ref, gain_f_ref, win_own, win_oth, wout_own, wout_oth, pt_own, pt_oth,
    x_hbm, xt_hbm, og_hbm, mid_hbm, start_hbm, yt_hbm, qkv_own_hbm, qkv_oth_hbm,
    mix_own_hbm, mix_oth_hbm, inv_own_hbm, inv_oth_hbm, wq_own_hbm, wk_own_hbm, wv_own_hbm, wq_oth_hbm, wk_oth_hbm,
    wv_oth_hbm, wo_own_hbm, wo_oth_hbm,
    result_ref, gtok_ref, out_in, out_out, out_q, out_k, out_v, out_o, out_small,
    x, xt, og, mid, qkv, mix, inv, gmix, wqkv, wo, feed, gnf, dst, dqkv, kaug, vaug, doaug,
    tacc, gvec, gains, ptb, g, xsend, xrecv, ring, load_sem, late_sem, pt_sem, out_sem, xs_sem, xr_sem,
    send_sem, recv_sem,
):
    s = pl.program_id(0)
    heads_half = n_heads // 2
    cols = heads_half * DH
    me = lax.axis_index("heads")
    early = [(x_hbm, x), (xt_hbm, xt), (og_hbm, og)]
    later = [
        (mid_hbm, mid),
        (qkv_own_hbm, qkv.at[0]),
        (qkv_oth_hbm, qkv.at[1]),
        (mix_own_hbm, mix.at[0]),
        (mix_oth_hbm, mix.at[1]),
        (inv_own_hbm, inv.at[0]),
        (inv_oth_hbm, inv.at[1]),
        (wq_own_hbm, wqkv.at[0, 0]),
        (wk_own_hbm, wqkv.at[0, 1]),
        (wv_own_hbm, wqkv.at[0, 2]),
        (wq_oth_hbm, wqkv.at[1, 0]),
        (wk_oth_hbm, wqkv.at[1, 1]),
        (wv_oth_hbm, wqkv.at[1, 2]),
        (wo_own_hbm, wo.at[0]),
        (wo_oth_hbm, wo.at[1]),
    ]
    n_early = len(early)
    loads = [
        pltpu.make_async_copy(a, b, load_sem.at[i]) for i, (a, b) in enumerate(early + later)
    ]
    late = [
        pltpu.make_async_copy(start_hbm, x, late_sem.at[0]),
        pltpu.make_async_copy(yt_hbm, xt, late_sem.at[1]),
    ]

    def pt_start(i):
        hh = 2 * (i // 4) + i % 2
        for o, ref in enumerate((pt_own, pt_oth)):

            @pl.when((i % 4) // 2 == o)
            def _():
                pltpu.make_async_copy(ref.at[hh], ptb.at[i % 2], pt_sem.at[i % 2]).start()

    n_out = cols // 128
    n_chunks = 2 * n_ff + 4 * n_out + 1
    n_units = n_chunks
    stages, n_halved, _ = plan_stages(n_rows)
    n_stages = len(stages)
    peers = stage_order(n_rows, 0)[2]
    core = {"heads": 1 - me}

    def swap(slot):
        return pltpu.make_async_remote_copy(
            src_ref=xsend.at[slot],
            dst_ref=xrecv.at[slot],
            send_sem=xs_sem.at[slot],
            recv_sem=xr_sem.at[slot],
            device_id=core,
            device_id_type=pl.DeviceIdType.MESH,
        )

    def emit(c, slot, own, oth):
        for blocks, ref in ((own, g.at[c]), (oth, xsend.at[slot])):
            for b, block in enumerate(blocks):
                n = block.shape[0]
                ref[b * n : (b + 1) * n, :] = block.astype(BF16)
        swap(slot).start()

    def collect(c, slot):
        swap(slot).wait()
        g[c] = (g[c].astype(F32) + xrecv[slot].astype(F32)).astype(BF16)

    def stage_copy(k, c):
        kind, j, n, slot = stages[k]
        pick, peer, _ = stage_order(n_rows, c % 2)
        base, size = 0, UNIT
        for i in range(min(j, n_halved)):
            size = size // 2
            base = base + pick[i] * size
        keep = base + pick[j] * n
        give = base + (1 - pick[j]) * n
        src, dst = {"halve": (give, keep), "swap": (base, base), "gather": (keep, give)}[kind]
        src, dst = (pl.ds(pl.multiple_of(r, 16), n) for r in (src, dst))
        par = c % SLOTS
        copy = pltpu.make_async_remote_copy(
            src_ref=g.at[c, src, :],
            dst_ref=ring.at[par, slot : slot + n, :],
            send_sem=send_sem.at[k, par],
            recv_sem=recv_sem.at[k, par],
            device_id={"rows": peer[j]},
            device_id_type=pl.DeviceIdType.MESH,
        )
        return copy, dst

    def stage_end(k, c):
        kind, _, n, slot = stages[k]
        copy, dst = stage_copy(k, c)
        copy.wait()
        part = ring[c % SLOTS, slot : slot + n, :]
        if kind != "gather":
            part = (g[c, dst, :].astype(F32) + part.astype(F32)).astype(BF16)
        g[c, dst, :] = part

    def out_wait(par):
        pltpu.make_async_copy(g.at[0], out_in.at[:, 0:128], out_sem.at[par]).wait()

    def out_start(c):
        sem = out_sem.at[c % 2]

        @pl.when(c >= 2)
        def _():
            out_wait(c % 2)

        def wide(ref, col):
            dst = ref.at[:, pl.ds(pl.multiple_of(col * 128, 128), 128)]
            pltpu.make_async_copy(g.at[c], dst, sem).start()

        def tall(ref, row):
            for b in range(D // 128):
                dst = ref.at[
                    pl.ds(pl.multiple_of(row * 128, 128), 128), b * 128 : (b + 1) * 128
                ]
                pltpu.make_async_copy(g.at[c, b * 128 : (b + 1) * 128], dst, sem).start()

        base = 2 * n_ff + n_out

        @pl.when(jnp.logical_and(c < 2 * n_ff, c % 2 == 0))
        def _():
            wide(out_in, c // 2)

        @pl.when(jnp.logical_and(c < 2 * n_ff, c % 2 == 1))
        def _():
            tall(out_out, c // 2)

        @pl.when(jnp.logical_and(c >= 2 * n_ff, c < base))
        def _():
            tall(out_o, c - 2 * n_ff)

        for m, ref in enumerate((out_q, out_k, out_v)):
            at = jnp.logical_and(c >= base, c < n_chunks - 1)

            @pl.when(jnp.logical_and(at, (c - base) % 3 == m))
            def _():
                wide(ref, (c - base) // 3)

        @pl.when(c == n_chunks - 1)
        def _():
            tall(out_small, 0)

    wo_end = 2 * n_ff + n_out
    holes = ((wo_end, 2), (wo_end + 5, 1))

    def tick(t):
        for k in range(n_stages, -1, -1):
            v = t - SPACING * k
            c = v
            valid = v >= 0
            for at, length in holes:
                c = c - jnp.where(v >= at + length, length, 0)
                valid = jnp.logical_and(valid, jnp.logical_or(v < at, v >= at + length))
            valid = jnp.logical_and(valid, c < n_units)

            @pl.when(valid)
            def _():
                if k > 0:
                    stage_end(k - 1, c)
                if k < n_stages:
                    stage_copy(k, c)[0].start()
                if k == n_stages:
                    out_start(c)

    def collect_ff(e):
        for j in range(2):
            collect(2 * e + j, 2 * (e % 4) + j)

    def group_slot(e, m):
        return 3 + m if e % 2 == 0 else m

    def collect_group(e):
        for m in range(3):
            collect((2 * n_ff + n_out + 3 * e + m), group_slot(e, m))

    def lanes(a):
        return [a[:, k : k + 128] for k in range(0, a.shape[1], 128)]

    @pl.when(s == 0)
    def _():
        for copy in loads:
            copy.start()
        barrier = pltpu.get_barrier_semaphore()
        for peer in [{"rows": p} for p in peers] + [core]:
            pl.semaphore_signal(
                barrier, inc=1, device_id=peer, device_id_type=pl.DeviceIdType.MESH
            )
        pl.semaphore_wait(barrier, len(peers) + 1)
        for copy in loads[:n_early]:
            copy.wait()
        feed[...] = jnp.zeros(feed.shape, F32)
        gnf[...] = jnp.zeros(gnf.shape, F32)

    @pl.when(s < n_ff)
    def _():
        wi = jnp.concatenate([win_own[...], win_oth[...]], axis=1)
        wout = jnp.concatenate([wout_own[...], wout_oth[...]], axis=0)
        halves = [slice(0, ROW // 2), slice(ROW // 2, ROW)]
        pres = [dot_nn(x[r, :], wi) for r in halves]
        gacts = [dot_nt(og[r, :], wout) for r in halves]
        acts, gpres = [], []
        for pre, gact in zip(pres, gacts):
            cdf = 0.5 * (1.0 + lax.erf(pre * ROOT_HALF))
            acts.append((pre * cdf).astype(BF16))
            slope = cdf + pre * jnp.exp(-0.5 * pre * pre) * DENSITY
            gpres.append((gact * slope).astype(BF16))
        for r, act, gpre in zip(halves, acts, gpres):
            feed[r, :] += dot_nn(act, wout)
            gnf[r, :] += dot_nt(gpre, wi)
        active = jnp.concatenate(acts, axis=0)
        gpre = jnp.concatenate(gpres, axis=0)

        @pl.when(s >= 2)
        def _():
            collect_ff(s - 2)
            tick(2 * (s - 2))

        dwin = dot_nn(xt[...], gpre)
        dwout = dot_tn(active, og[...])

        emit(2 * s, 2 * (s % 4), [dwin[:, :FFC]], [dwin[:, FFC:]])
        emit(2 * s + 1, 2 * (s % 4) + 1, lanes(dwout[:FFC]), lanes(dwout[FFC:]))

        @pl.when(s >= 2)
        def _():
            tick(2 * (s - 2) + 1)

    @pl.when(s == n_ff)
    def _():
        for copy in late:
            copy.start()
        pt_start(0)
        for copy in loads[n_early:]:
            copy.wait()
        collect_ff(n_ff - 2)
        t0 = 2 * (n_ff - 2)
        tick(t0)
        middle = mid[...]
        result_ref[...] = (middle + feed[...]).astype(BF16)
        back, gain_grad = norm_back(middle, gain_f_ref[...][None, :], gnf[...])
        gmid = og[...].astype(F32) + back
        gains[0:1, :] = gain_grad
        mid[...] = gmid
        tick(t0 + 1)
        ga = gmid.astype(BF16)
        dwo = [dot_nn(mix[o], ga) for o in range(2)]
        collect_ff(n_ff - 1)
        for j in range(n_out):
            rows = slice(j * 128, (j + 1) * 128)
            emit((2 * n_ff + j), j, lanes(dwo[0][rows]), lanes(dwo[1][rows]))
        for o in range(2):
            grad = dot_nt(wo[o], ga)
            for k in range(heads_half):
                rows = slice(k * DH, (k + 1) * DH)
                gmix[o, rows, :] = (grad[rows] * inv[o, k : k + 1, :]).astype(BF16)
        tick(t0 + 2)
        gnf[...] = jnp.zeros(gnf.shape, F32)
        kaug[DH:, :] = key_marks(own_row(seg_ref))
        vaug[DH:, :] = (iota((16, ROW), 0) < 3).astype(F32).astype(BF16)
        gvec[...] = jnp.zeros(gvec.shape, F32)
        for copy in late:
            copy.wait()
        tick(t0 + 3)

    i = s - (n_ff + 1)

    def head_back(o, pt_ref):
        hh = 2 * (i // 4) + i % 2
        rows = pl.ds(pl.multiple_of(hh * DH, DH), DH)
        dot_ = gmix[o, rows, :]
        delta = jnp.sum(dot_.astype(F32) * mix[o, rows, :].astype(F32), axis=0, keepdims=True)
        d1 = delta.astype(BF16).astype(F32)
        d2 = (delta - d1).astype(BF16).astype(F32)
        d3 = delta - d1 - d2
        k = iota((16, ROW), 0)
        vaug[0:DH, :] = qkv[o, 2, rows, :]
        kaug[0:DH, :] = qkv[o, 1, rows, :]
        doaug[0:DH, :] = dot_
        doaug[DH:, :] = jnp.where(
            k == 0, -d1, jnp.where(k == 1, -d2, jnp.where(k == 2, -d3, 0.0))
        ).astype(BF16)
        va = vaug[...]
        ka = kaug[...]
        out_rows = pl.ds(pl.multiple_of(o * 128 + (i % 2) * DH, DH), DH)
        tacc[...] = jnp.zeros(tacc.shape, F32)
        left = jnp.zeros((1, QB), F32)
        right = jnp.zeros((1, QB), F32)
        n_blocks = ROW // QB

        def grad_probs(b):
            return dot_tn(va, doaug[:, b * QB : (b + 1) * QB])

        dp = grad_probs(0)
        dqkv[2, out_rows, :] = dot_nt(dot_, pt_ref[...]).astype(BF16)
        for b in range(n_blocks):
            qs = slice(b * QB, (b + 1) * QB)
            ahead = grad_probs(b + 1) if b + 1 < n_blocks else None
            ds = pt_ref[:, qs].astype(F32) * dp
            for u in range(QB // BT):
                qb = b * (QB // BT) + u
                for d in (-1, 0, 1):
                    kb = qb + d
                    if 0 <= kb < NBLK:
                        tacc[:, 256 - 128 * d : 384 - 128 * d] += ds[
                            kb * BT : (kb + 1) * BT, u * BT : (u + 1) * BT
                        ]
            dst[:, qs] = ds.astype(BF16)
            dp = ahead
        for b in range(n_blocks):
            qs = slice(b * QB, (b + 1) * QB)
            r = dot_nn(ka, dst[:, qs])
            dqkv[0, out_rows, qs] = r[:DH].astype(BF16)
            sums = r[DH + 8 :]
            j = iota((8, QB), 0)
            block = b * (QB // BT) + iota((8, QB), 1) // BT
            left = left + jnp.sum(jnp.where(j <= block - 2, sums, 0.0), axis=0, keepdims=True)
            right = right + jnp.sum(jnp.where(j >= block + 2, sums, 0.0), axis=0, keepdims=True)
        dqkv[1, out_rows, :] = dot_nt(qkv[o, 0, rows, :], dst[...]).astype(BF16)
        flip = (iota((BT, BT), 0) + iota((BT, BT), 1) == BT - 1).astype(F32).astype(BF16)
        near = tacc[...]
        high = near.astype(BF16)
        low = (near - high.astype(F32)).astype(BF16)
        turned = dot_nn(flip, high) + dot_nn(flip, low)
        skew = pltpu.roll(turned, 0, 1, stride=1, stride_axis=0)
        vec = pltpu.roll(jnp.sum(skew, axis=0, keepdims=True), 512 - (BT - 1), 1)
        lane = iota((1, 512), 1)
        vec = vec + jnp.where(lane == 511, jnp.sum(left, axis=1, keepdims=True), 0.0)
        vec = vec + jnp.where(lane == 1, jnp.sum(right, axis=1, keepdims=True), 0.0)
        owner = me + o * (1 - 2 * me)
        gvec[pl.ds(owner * heads_half + hh, 1), :] = vec

    in_heads = jnp.logical_and(i >= 0, i < n_heads)

    @pl.when(in_heads)
    def _():
        @pl.when(i + 1 < n_heads)
        def _():
            pt_start(i + 1)

        pltpu.make_async_copy(pt_own.at[0], ptb.at[i % 2], pt_sem.at[i % 2]).wait()
        head_back((i % 4) // 2, ptb.at[i % 2])

        @pl.when(i == 0)
        def _():
            for j in range(n_out):
                collect((2 * n_ff + j), j)

        for e in range(n_heads // 4 - 1):

            @pl.when(i == 4 * (e + 1) + 1)
            def _():
                collect_group(e)

        tick(2 * n_ff + i)

    def group_back(grp):
        for m in range(3):
            grad = dqkv[m]
            dw = dot_nt(xt[...], grad)
            emit(
                (2 * n_ff + n_out + 3 * grp + m), group_slot(grp, m),
                [dw[:, :128]], [dw[:, 128:]],
            )
            cols_g = slice(grp * 128, (grp + 1) * 128)
            w = jnp.concatenate([wqkv[0, m, :, cols_g], wqkv[1, m, :, cols_g]], axis=1)
            part = lax.dot_general(grad, w, (((0,), (1,)), ((), ())), preferred_element_type=F32)
            gnf[...] += part

    for grp in range(n_heads // 4):

        @pl.when(i == 4 * grp + 3)
        def _():
            group_back(grp)

    @pl.when(i == n_heads)
    def _():
        seg = own_row(seg_ref)
        start = x[...].astype(F32)
        back, gain_grad = norm_back(start, gain_a_ref[...][None, :], gnf[...])
        gstart = mid[...] + back
        n_groups = n_heads // 4
        collect_group(n_groups - 1)
        t0 = 2 * n_ff + n_heads
        tick(t0)
        picks = picks_t(seg)
        here = dot_tn(picks, (iota((128, 128), 0) < PROMPT).astype(F32).astype(BF16)) > 0.5
        for c in range(0, D, 128):
            gtok_ref[:, c : c + 128] = jnp.where(here, 0.0, gstart[:, c : c + 128]).astype(BF16)
        high = gstart.astype(BF16)
        low = (gstart - high.astype(F32)).astype(BF16)
        tick(t0 + 1)
        gprompt = dot_nn(picks, high) + dot_nn(picks, low)
        opicks = offset_picks(128).astype(BF16)
        gv = gvec[...]
        g1 = gv.astype(BF16)
        g2 = (gv - g1.astype(F32)).astype(BF16)
        gtab = dot_nt(g1, opicks) + dot_nt(g2, opicks)
        row = iota((128, D), 0)
        small = jnp.where(row < PROMPT, gprompt, 0.0)
        small = jnp.where(row == PROMPT, gain_grad, small)
        small = jnp.where(row == PROMPT + 1, gains[0:1, :], small)
        blocks = lanes(small)
        wide = jnp.concatenate([jnp.zeros((104, 128), F32), gtab, jnp.zeros((8, 128), F32)], axis=0)
        blocks[0] = blocks[0] + wide
        slot = group_slot(n_groups, 0)
        emit((n_chunks - 1), slot, blocks, blocks)
        tick(t0 + 2)
        collect((n_chunks - 1), slot)

        @pl.loop(t0 + 3, n_units + sum(h[1] for h in holes) + SPACING * n_stages)
        def _(t):
            tick(t)

        out_wait(0)
        out_wait(1)


def run_backward(
    n_rows, seg, gain_a, gain_f, win_own, win_oth, wout_own, wout_oth, pt_own, pt_oth, rest
):
    n_ff = win_own.shape[1] // FFC
    n_heads = 2 * pt_own.shape[0]
    cols = n_heads * DH // 2
    n_chunks = 2 * n_ff + 4 * (cols // 128) + 1
    first = n_ff + 1
    stages, _, ring_rows = plan_stages(n_rows)
    n_stages = len(stages)

    def ff(s):
        return jnp.minimum(s, n_ff - 1)

    blk_in = pl.BlockSpec((D, FFC), lambda s: (0, ff(s)))
    blk_out = pl.BlockSpec((FFC, D), lambda s: (ff(s), 0))
    anyspec = pl.BlockSpec(memory_space=pl.ANY)
    return pl.pallas_call(
        partial(backward, n_ff, n_heads, n_rows),
        grid=(first + n_heads + 1,),
        in_specs=[
            whole(seg.shape), whole(gain_a.shape), whole(gain_f.shape),
            blk_in, blk_in, blk_out, blk_out,
        ] + [anyspec] * (2 + len(rest)),
        out_specs=[whole((ROW, D)), whole((ROW, D))] + [anyspec] * 7,
        out_shape=[sds((ROW, D), BF16), sds((ROW, D), BF16)] + [
            sds(shape, BF16)
            for shape in (win_own.shape, wout_own.shape)
            + ((D, cols),) * 3 + ((cols, D), (128, D))
        ],
        scratch_shapes=[
            pltpu.VMEM((ROW, D), BF16),
            pltpu.VMEM((D, ROW), BF16),
            pltpu.VMEM((ROW, D), BF16),
            pltpu.VMEM((ROW, D), F32),
            pltpu.VMEM((2, 3, cols, ROW), BF16),
            pltpu.VMEM((2, cols, ROW), BF16),
            pltpu.VMEM((2, 8, ROW), F32),
            pltpu.VMEM((2, cols, ROW), BF16),
            pltpu.VMEM((2, 3, D, cols), BF16),
            pltpu.VMEM((2, cols, D), BF16),
            pltpu.VMEM((ROW, D), F32),
            pltpu.VMEM((ROW, D), F32),
            pltpu.VMEM((ROW, ROW), BF16),
            pltpu.VMEM((3, 256, ROW), BF16),
            pltpu.VMEM((DH + 16, ROW), BF16),
            pltpu.VMEM((DH + 16, ROW), BF16),
            pltpu.VMEM((DH + 16, ROW), BF16),
            pltpu.VMEM((BT, 512), F32),
            pltpu.VMEM((16, 512), F32),
            pltpu.VMEM((8, D), F32),
            pltpu.VMEM((2, ROW, ROW), BF16),
            pltpu.VMEM((n_chunks, UNIT, 128), BF16),
            pltpu.VMEM((8, CH, 128), BF16),
            pltpu.VMEM((8, CH, 128), BF16),
            pltpu.VMEM((SLOTS, ring_rows, 128), BF16),
            pltpu.SemaphoreType.DMA((18,)),
            pltpu.SemaphoreType.DMA((2,)),
            pltpu.SemaphoreType.DMA((2,)),
            pltpu.SemaphoreType.DMA((2,)),
            pltpu.SemaphoreType.DMA((8,)),
            pltpu.SemaphoreType.DMA((8,)),
            pltpu.SemaphoreType.DMA((n_stages, SLOTS)),
            pltpu.SemaphoreType.DMA((n_stages, SLOTS)),
        ],
        compiler_params=pltpu.CompilerParams(
            vmem_limit_bytes=62 * 1024 * 1024, collective_id=0, has_side_effects=True
        ),
        name="backward",
    )(seg, gain_a, gain_f, win_own, win_oth, wout_own, wout_oth, pt_own, pt_oth, *rest)


def finish(
    heads, result, gtok, small, g_q, g_k, g_v, g_wo, g_in, g_out,
    o_result, o_gtok, o_prompt, o_gain_a, o_q, o_k, o_v, o_wo, o_tab, o_gain_f, o_in, o_out, rows,
):
    o_result[...] = result[...]
    o_gtok[...] = gtok[...]
    for src, dst in ((g_q, o_q), (g_k, o_k), (g_v, o_v), (g_wo, o_wo), (g_in, o_in), (g_out, o_out)):
        dst[...] = src[...].astype(F32)

    @pl.when(pl.program_id(0) == 0)
    def _():
        rows[...] = small[...].astype(F32)
        o_prompt[...] = rows[0:PROMPT, :]
        o_gain_a[...] = rows[PROMPT, :]
        o_gain_f[...] = rows[PROMPT + 1, :]
        low = lax.axis_index("heads") == 0
        at = 104
        tab = [
            jnp.where(low, rows[at + k : at + k + 1, 0:128], rows[at + heads + k : at + heads + k + 1, 0:128])
            for k in range(heads)
        ]
        tab.append(jnp.zeros((8 - heads, 128), F32))
        o_tab[...] = jnp.concatenate(tab, axis=0).T[0:NB, 0:heads]


def run_finish(heads, result, gtok, small, *grads):
    steps = 8

    def part(a):
        return pl.BlockSpec((a.shape[0] // steps, a.shape[1]), lambda i: (i, 0))

    g_q, g_k, g_v, g_wo, g_in, g_out = grads
    whole_1d = pl.BlockSpec((D,), lambda i: (0,))
    return pl.pallas_call(
        partial(finish, heads),
        grid=(steps,),
        in_specs=[part(result), part(gtok), whole(small.shape)] + [part(a) for a in grads],
        out_specs=[part(result), part(gtok), whole_out((PROMPT, D)), whole_1d]
        + [part(a) for a in (g_q, g_k, g_v, g_wo)]
        + [whole_out((NB, heads)), whole_1d, part(g_in), part(g_out)],
        out_shape=[sds(result.shape, BF16), sds(gtok.shape, BF16), sds((PROMPT, D), F32), sds((D,), F32)]
        + [sds(a.shape, F32) for a in (g_q, g_k, g_v, g_wo)]
        + [sds((NB, heads), F32), sds((D,), F32), sds(g_in.shape, F32), sds(g_out.shape, F32)],
        scratch_shapes=[pltpu.VMEM((128, D), F32)],
        compiler_params=pltpu.CompilerParams(vmem_limit_bytes=62 * 1024 * 1024),
        name="finish",
    )(result, gtok, small, *grads)


def on_device(
    tokens, prompt, segment_ids, gain_attn, w_query, w_key, w_value, w_attn_out, bias_table,
    gain_ff, w_in, w_out, out_grad,
):
    seg = segment_ids
    swap = [(0, 1), (1, 0)]

    def other(a):
        return lax.ppermute(a, "heads", swap)

    tab_oth, wq_oth, wk_oth, wv_oth = (other(a) for a in (bias_table, w_query, w_key, w_value))
    wo_oth, win_oth, wout_oth = other(w_attn_out), other(w_in), other(w_out)
    gain_a, gain_f = gain_attn, gain_ff
    start, yt, qkv_own, pt_own, mix_own, inv_own = run_first(
        seg, tokens, prompt, gain_a, w_query, w_key, w_value, bias_table
    )
    qkv_oth, pt_oth, mix_oth, inv_oth, middle, x, xt = run_second(
        seg, start, yt, gain_f, wq_oth, wk_oth, wv_oth, tab_oth, mix_own, w_attn_out, wo_oth
    )
    result, gtok, g_in, g_out, g_q, g_k, g_v, g_wo, small = run_backward(
        lax.axis_size("rows"),
        seg, gain_a, gain_f, w_in, win_oth, w_out, wout_oth, pt_own, pt_oth,
        [x, xt, out_grad, middle, start, yt, qkv_own, qkv_oth, mix_own, mix_oth,
         inv_own, inv_oth,
         w_query, w_key, w_value, wq_oth, wk_oth, wv_oth, w_attn_out, wo_oth],
    )
    (
        result, gtok, g_prompt, g_gain_a, g_q, g_k, g_v, g_wo, g_tab, g_gain_f, g_in, g_out,
    ) = run_finish(bias_table.shape[1], result, gtok, small, g_q, g_k, g_v, g_wo, g_in, g_out)
    return (
        result, gtok, g_prompt, g_gain_a, g_q, g_k, g_v, g_wo, g_tab, g_gain_f, g_in, g_out,
    )


def solution(mesh):
    both = P(("rows", "heads"), None)
    cols = P(None, "heads")
    rows = P("heads", None)
    in_specs = (
        both, P(), P("rows", None), P(), cols, cols, cols, rows, cols, P(), cols, rows, both,
    )
    out_specs = (both, both, P(), P(), cols, cols, cols, rows, cols, P(), cols, rows)
    return jax.shard_map(
        on_device, mesh=mesh, in_specs=in_specs, out_specs=out_specs, check_vma=False
    )
```

time: 314 us -> 225 us (0.72)
  Pallas kernels: 284 us -> 220 us
  other arithmetic: 12.4 us -> 0 us
  local copies, waits for them, and re-layouts: 11.1 us -> 3.34 us
  waiting for transfers between devices: 3.99 us -> 0.17 us
    pallas_call x1, Pallas kernels: 222 us -> 166 us  [run_backward(): pl.pallas_call(partial(backward, n_ff, n_heads, n_rows), grid=(first + n_...]
    convert_element_type x7 -> x0, other arithmetic: 10.7 us -> none  [on_device(): a.astype(F32)]
    pallas_call x2 -> x3, Pallas kernels: 61.7 us -> 53.6 us  [the longest x1 22.6 us: run_second(): pl.pallas_call(forward_second, grid=(heads // GROUP, ROW // QB), in_specs...]
    ppermute x7, waiting for transfers between devices: 3.99 us -> 0.17 us  [other(): return lax.ppermute(a, 'heads', swap)]
  transfers between devices with their start and end apart: 7 -> 7, of which waited for: 2 -> 1; matrix products, arithmetic and copies ran while one was open for 2% -> 0% of each run, Pallas kernels for 20% -> 18%
where the time goes in v1:
time: 225 us; the launch traced here: 226 us
  Pallas kernels  220 us (98%)
  local copies, waits for them, and re-layouts  3.34 us (1%)
    pallas_call x1, Pallas kernels, run_backward(): pl.pallas_call(partial(backward, n_ff, n_heads, n_rows), grid=(first + n_...  166 us
    pallas_call x1, Pallas kernels, run_second(): pl.pallas_call(forward_second, grid=(heads // GROUP, ROW // QB), in_specs...  22.6 us
    pallas_call x1, Pallas kernels, run_first(): pl.pallas_call(forward_first, grid=(heads // GROUP, ROW // QB), in_specs=...  19.2 us
    pallas_call x1, Pallas kernels, run_finish(): pl.pallas_call(partial(finish, heads), grid=(steps,), in_specs=[part(resu...  11.9 us
  transfers between devices with their start and end apart: 7, of which 1 were waited for; matrix products, arithmetic and copies ran while one was open for 0% of the time, Pallas kernels for 18%

profile of v1, /device:TPU:0, one launch (start us, length us, event | category | flops | bytes accessed | tf_op | source)
XLA Modules:
  0.0 226.3 jit_solution(10507501042782375971)
XLA Ops:
  0.6 0.5 collective-permute-start.2
  1.2 0.8 copy.25.tab_ref
  1.9 0.1 collective-permute-start.5
  2.0 0.5 collective-permute-start.3
  2.5 0.1 collective-permute-start.4
  2.6 0.4 collective-permute-start.6
  3.0 0.2 collective-permute-done.5.tab_ref
  3.1 0.2 collective-permute-start
  3.3 0.0 collective-permute-done.2.wq.wq_oth_hbm
  3.3 0.3 collective-permute-start.1
  3.7 19.2 %attend_own.1 = (bf16[1024,768]{1,0:T(8,128)(2,1)}, bf16[768,1024]{1,0:T(8,128)(2,1)}, bf16[3,384,1024]{2,1,0:T(8,128)(2,1)}, bf16[6,1024,1024]{2,1,0:T(8,128)(2...) custom-call(s32[2,1024]{1,0:T(2,128)} %seg_ref.5, bf16[1024,768]{1,0:T(8,128)(2,1)} %tok_ref.1, ...), custom_call_target="tpu_custom_call" | custom-call | flops 20000000000 | bytes 10000000 | tf_op jit(solution)/shard_map/attend_own/pallas_call | solution.py:307
  22.8 0.0 collective-permute-done.3.wk.wk_oth_hbm
  22.8 0.0 copy-start.1
  22.9 0.0 collective-permute-done.4.wv.wv_oth_hbm
  22.9 0.0 collective-permute-done.6.wo_oth.wo_oth_hbm
  22.9 0.8 copy-done.1
  23.7 0.2 copy-done.2
  23.9 0.2 copy-done.3
  24.1 22.6 %attend_other.1 = (bf16[3,384,1024]{2,1,0:T(8,128)(2,1)}, bf16[6,1024,1024]{2,1,0:T(8,128)(2,1)}, bf16[384,1024]{1,0:T(8,128)(2,1)}, f32[8,1024]{1,0:T(8,128)}, ...) custom-call(s32[2,1024]{1,0:T(2,128)} %seg_ref.5, ...), custom_call_target="tpu_custom_call" | custom-call | flops 20000000000 | bytes 10000000 | tf_op jit(solution)/shard_map/attend_other/pallas_call | solution.py:338
  46.7 0.0 collective-permute-done.win_oth
  46.7 0.0 collective-permute-done.1.wout_oth
  46.7 166.1 %backward.1 = (bf16[1024,768]{1,0:T(8,128)(2,1)}, bf16[1024,768]{1,0:T(8,128)(2,1)}, bf16[768,1536]{1,0:T(8,128)(2,1)}, bf16[1536,768]{1,0:T(8,128)(2,1)}, bf16[...) custom-call(s32[2,1024]{1,0:T(2,128)} %seg_ref.5, ...), custom_call_target="tpu_custom_call" | custom-call | tf_op jit(solution)/shard_map/backward/pallas_call | solution.py:823
  212.8 11.9 %finish.1 = (bf16[1024,768]{1,0:T(8,128)(2,1)}, bf16[1024,768]{1,0:T(8,128)(2,1)}, f32[100,768]{1,0:T(8,128)}, f32[768]{0:T(1024)}, f32[768,384]{1,0:T(8,128)}, ...) custom-call(bf16[1024,768]{1,0:T(8,128)(2,1)} %get-tuple-element.47., ...), custom_call_target="tpu_custom_call" | custom-call | tf_op jit(solution)/shard_map/finish/pallas_call | solution.py:911
  224.7 1.4 copy.27
  (8 shorter events, 0.0 us)
Async XLA Ops:
  0.6 2.7 %collective-permute-start.2 = (bf16[768,384]{1,0:T(8,128)(2,1)}, bf16[768,384]{1,0:T(8,128)(2,1)S(1)}, u32[]{:S(2)}, u32[]{:S(2)}) collective-permute-start(bf16[768,384]{1,0:T(8,128)(2,1)} %wq_own_hbm.1), channel_id=1, source_target_pairs={{0,1},{1,0},{2,3},{3,2},{4,5},{5,4},{6,7},{7,6},{8,9},{9,8},{10,11... | collective-permute-start | bytes 1769480 | tf_op jit(solution)/shard_map/ppermute | solution.py:935
  1.9 1.7 copy-start.4
  1.9 1.2 collective-permute-start.5
  2.0 20.8 %collective-permute-start.3 = (bf16[768,384]{1,0:T(8,128)(2,1)}, bf16[768,384]{1,0:T(8,128)(2,1)S(1)}, u32[]{:S(2)}, u32[]{:S(2)}) collective-permute-start(bf16[768,384]{1,0:T(8,128)(2,1)} %wk_own_hbm.1), channel_id=1, source_target_pairs={{0,1},{1,0},{2,3},{3,2},{4,5},{5,4},{6,7},{7,6},{8,9},{9,8},{10,11... | collective-permute-start | bytes 1769480 | tf_op jit(solution)/shard_map/ppermute | solution.py:935
  2.5 20.4 %collective-permute-start.4 = (bf16[768,384]{1,0:T(8,128)(2,1)}, bf16[768,384]{1,0:T(8,128)(2,1)S(1)}, u32[]{:S(2)}, u32[]{:S(2)}) collective-permute-start(bf16[768,384]{1,0:T(8,128)(2,1)} %wv_own_hbm.1), channel_id=1, source_target_pairs={{0,1},{1,0},{2,3},{3,2},{4,5},{5,4},{6,7},{7,6},{8,9},{9,8},{10,11... | collective-permute-start | bytes 1769480 | tf_op jit(solution)/shard_map/ppermute | solution.py:935
  2.6 20.3 %collective-permute-start.6 = (bf16[384,768]{1,0:T(8,128)(2,1)}, bf16[384,768]{1,0:T(8,128)(2,1)S(1)}, u32[]{:S(2)}, u32[]{:S(2)}) collective-permute-start(bf16[384,768]{1,0:T(8,128)(2,1)} %wo_own_hbm.1), channel_id=1, source_target_pairs={{0,1},{1,0},{2,3},{3,2},{4,5},{5,4},{6,7},{7,6},{8,9},{9,8},{10,11... | collective-permute-start | bytes 1769480 | tf_op jit(solution)/shard_map/ppermute | solution.py:935
  3.1 19.7 %copy-start.5 = (bf16[32,6]{1,0:T(8,128)(2,1)}, bf16[32,6]{1,0:T(8,128)(2,1)S(1)}, u32[]{:S(2)}) copy-start(bf16[32,6]{1,0:T(8,128)(2,1)S(1)} %collective-permute-done.5.tab_ref) | copy-start | bytes 1156
  3.1 43.5 %collective-permute-start = (bf16[768,1536]{1,0:T(8,128)(2,1)}, bf16[768,1536]{1,0:T(8,128)(2,1)}, u32[]{:S(2)}, u32[]{:S(2)}) collective-permute-start(bf16[768,1536]{1,0:T(8,128)(2,1)} %win_own.1), channel_id=1, source_target_pairs={{0,1},{1,0},{2,3},{3,2},{4,5},{5,4},{6,7},{7,6},{8,9},{9,8},{10,11... | collective-permute-start | bytes 7077896 | tf_op jit(solution)/shard_map/ppermute | solution.py:935
  3.3 19.5 %copy-start = (bf16[768,384]{1,0:T(8,128)(2,1)}, bf16[768,384]{1,0:T(8,128)(2,1)S(1)}, u32[]{:S(2)}) copy-start(bf16[768,384]{1,0:T(8,128)(2,1)S(1)} %collective-permute-done.2.wq.wq_oth_hbm) | copy-start | bytes 1769476
  3.3 43.4 %collective-permute-start.1 = (bf16[1536,768]{1,0:T(8,128)(2,1)}, bf16[1536,768]{1,0:T(8,128)(2,1)}, u32[]{:S(2)}, u32[]{:S(2)}) collective-permute-start(bf16[1536,768]{1,0:T(8,128)(2,1)} %wout_own.1), channel_id=1, source_target_pairs={{0,1},{1,0},{2,3},{3,2},{4,5},{5,4},{6,7},{7,6},{8,9},{9,8},{10,11... | collective-permute-start | bytes 7077896 | tf_op jit(solution)/shard_map/ppermute | solution.py:935
  22.8 0.8 copy-start.1
  22.9 1.0 copy-start.2
  22.9 1.2 copy-start.3

commit v2 on v1

--- a/solution.py
+++ b/solution.py
@@ -24,10 +24,11 @@
 CH = 768
 UNIT = CH
 QB = 256
+LONGEST = ROW - 3 * 128
 GROUP = 3
 SIZES = (2, 3, 4, 5, 6, 8)
 SPACING = 3
-SLOTS = 7
+SLOTS = 8
 BT = 128
 NBLK = ROW // BT
 
@@ -160,8 +161,8 @@
 
 def head_setup(seg, tab_ref, table_f, span, kaug, qaug, vaug, strip):
     picks = offset_picks(NB).astype(BF16)
-    wide_tab = jnp.concatenate([tab_ref[...], jnp.zeros((NB, 128 - tab_ref.shape[1]), BF16)], axis=1)
-    table_f[...] = dot_tn(wide_tab, picks)[0:8]
+    heads = tab_ref.shape[0]
+    table_f[0:heads, :] = dot_nn(tab_ref[...], picks)
     kaug[DH:, :] = jnp.zeros((128 - DH, ROW), BF16)
     qaug[:, DH:, :] = jnp.zeros((GROUP, 128 - DH, ROW), BF16)
     kaug[DH : DH + 16, :] = key_marks(seg)
@@ -180,8 +181,12 @@
 def forward_first(
     seg_ref, tok_ref, prompt_ref, gain_ref, wq, wk, wv, tab_ref,
     start_ref, yt_ref, qkv_ref, pt_ref, mixed_ref, inv_ref,
-    table_f, span, kaug, qaug, vaug, kn, strip, padded,
+    table_f, span, kaug, qaug, vaug, kn, strip, padded, start_s, yt_s, qkv_s, sem,
 ):
+    copies = [
+        pltpu.make_async_copy(a, b, sem.at[k])
+        for k, (a, b) in enumerate(((start_s, start_ref), (yt_s, yt_ref), (qkv_s, qkv_ref)))
+    ]
     step, q = pl.program_id(0), pl.program_id(1)
     first = jnp.logical_and(step == 0, q == 0)
     seg = own_row(seg_ref)
@@ -201,45 +206,67 @@
             ],
             axis=1,
         )
-        start_ref[...] = start.astype(BF16)
+        start_s[...] = start.astype(BF16)
+        copies[0].start()
         inv = lax.rsqrt(jnp.mean(start * start, axis=1, keepdims=True) + EPS)
         yt = (start * inv * gain_ref[...][None, :]).astype(BF16).T
-        yt_ref[...] = yt
-        project_t((wq, wk, wv), yt, qkv_ref)
+        yt_s[...] = yt
+        copies[1].start()
+        project_t((wq, wk, wv), yt, qkv_s)
+        copies[2].start()
         head_setup(seg, tab_ref, table_f, span, kaug, qaug, vaug, strip)
 
     attend_heads(
-        step, q, seg, table_f, span, qkv_ref, kaug, qaug, vaug, kn, strip, pt_ref, mixed_ref, inv_ref
+        step, q, seg, table_f, span, qkv_s, kaug, qaug, vaug, kn, strip, pt_ref, mixed_ref, inv_ref
     )
+
+    @pl.when(jnp.logical_and(step == pl.num_programs(0) - 1, q == pl.num_programs(1) - 1))
+    def _():
+        for copy in copies:
+            copy.wait()
 
 
 def forward_second(
     seg_ref, start_ref, yt_ref, gain_ref, wq, wk, wv, tab_ref, mixed_own, wo_own, wo_oth,
     qkv_ref, pt_ref, mixed_ref, inv_ref, middle_ref, x_ref, xt_ref,
-    table_f, span, kaug, qaug, vaug, kn, strip,
+    table_f, span, kaug, qaug, vaug, kn, strip, qkv_s, middle_s, x_s, xt_s, sem,
 ):
+    qkv_copy = pltpu.make_async_copy(qkv_s, qkv_ref, sem.at[0])
     step, q = pl.program_id(0), pl.program_id(1)
     first = jnp.logical_and(step == 0, q == 0)
     seg = own_row(seg_ref)
 
     @pl.when(first)
     def _():
-        project_t((wq, wk, wv), yt_ref[...], qkv_ref)
+        project_t((wq, wk, wv), yt_ref[...], qkv_s)
+        qkv_copy.start()
         head_setup(seg, tab_ref, table_f, span, kaug, qaug, vaug, strip)
 
     attend_heads(
-        step, q, seg, table_f, span, qkv_ref, kaug, qaug, vaug, kn, strip, pt_ref, mixed_ref, inv_ref
+        step, q, seg, table_f, span, qkv_s, kaug, qaug, vaug, kn, strip, pt_ref, mixed_ref, inv_ref
     )
 
     @pl.when(jnp.logical_and(step == pl.num_programs(0) - 1, q == pl.num_programs(1) - 1))
     def _():
-        attn = dot_tn(mixed_own[...], wo_own[...]) + dot_tn(mixed_ref[...], wo_oth[...])
-        middle = start_ref[...].astype(F32) + attn
-        middle_ref[...] = middle
-        inv = lax.rsqrt(jnp.mean(middle * middle, axis=1, keepdims=True) + EPS)
-        x = (middle * inv * gain_ref[...][None, :]).astype(BF16)
-        x_ref[...] = x
-        xt_ref[...] = x.T
+        copies = []
+        for k in range(0, ROW, QB):
+            r = slice(k, k + QB)
+            attn = dot_tn(mixed_own[:, r], wo_own[...]) + dot_tn(mixed_ref[:, r], wo_oth[...])
+            middle = start_ref[r, :].astype(F32) + attn
+            middle_s[r, :] = middle
+            inv = lax.rsqrt(jnp.mean(middle * middle, axis=1, keepdims=True) + EPS)
+            x = (middle * inv * gain_ref[...][None, :]).astype(BF16)
+            x_s[r, :] = x
+            xt_s[:, r] = x.T
+            for src, dst in ((middle_s, middle_ref), (x_s, x_ref)):
+                copies.append((src.at[r, :], dst.at[r, :]))
+            copies.append((xt_s.at[:, r], xt_ref.at[:, r]))
+            for m in range(3):
+                at = 3 * (k // QB) + m
+                pltpu.make_async_copy(*copies[at], sem.at[1 + at]).start()
+        qkv_copy.wait()
+        for at, pair in enumerate(copies):
+            pltpu.make_async_copy(*pair, sem.at[1 + at]).wait()
 
 
 def plan_stages(n_rows):
@@ -260,16 +287,32 @@
     return stages, len(halved), slot
 
 
-def stage_order(n_rows, odd):
+def stage_table(n_rows):
+    stages, n_halved, _ = plan_stages(n_rows)
     n_bits = n_rows.bit_length() - 1
     me = lax.axis_index("rows")
     bits = [(me // (1 << b)) % 2 for b in range(n_bits)]
     peers = [me + (1 - 2 * bits[b]) * (1 << b) for b in range(n_bits)]
-    even = [0, 2, 1] + list(range(3, n_bits))
-    flip = [1, 2, 0] + list(range(3, n_bits))
-    pick = [(bits[a] + odd * (bits[b] - bits[a])) for a, b in zip(even, flip)]
-    peer = [(peers[a] + odd * (peers[b] - peers[a])) for a, b in zip(even, flip)]
-    return pick, peer, peers
+    rest = list(range(3, n_bits))
+    sides = []
+    for order in ([0, 2, 1] + rest, [1, 2, 0] + rest):
+        bases, base, size = [], 0, UNIT
+        for j in range(n_bits):
+            bases.append(base)
+            if j < n_halved:
+                size = size // 2
+                base = base + bits[order[j]] * size
+        side = []
+        for kind, j, n, _ in stages:
+            keep = bases[j] + bits[order[j]] * n
+            give = bases[j] + (1 - bits[order[j]]) * n
+            src, dst = {
+                "halve": (give, keep), "swap": (bases[j], bases[j]), "gather": (keep, give)
+            }[kind]
+            side.append((src, dst, peers[order[j]]))
+        sides.append(side)
+    table = [(kind, n, slot, sides[0][k], sides[1][k]) for k, (kind, _, n, slot) in enumerate(stages)]
+    return table, peers
 
 
 def whole(shape):
@@ -309,9 +352,9 @@
         grid=(heads // GROUP, ROW // QB),
         in_specs=[whole(a.shape) for a in (seg, tok, prompt, gain, wq, wk, wv, tab)],
         out_specs=[
-            whole_out((ROW, D)),
-            whole_out((D, ROW)),
-            whole_out((3, cols, ROW)),
+            pl.BlockSpec(memory_space=pl.ANY),
+            pl.BlockSpec(memory_space=pl.ANY),
+            pl.BlockSpec(memory_space=pl.ANY),
             pl.BlockSpec((GROUP, ROW, QB), lambda h, q: (h, 0, q)),
             whole_out((cols, ROW)),
             whole_out((8, ROW)),
@@ -324,7 +367,13 @@
             sds((cols, ROW), BF16),
             sds((8, ROW), F32),
         ],
-        scratch_shapes=forward_scratch() + [pltpu.VMEM((128, D), BF16)],
+        scratch_shapes=forward_scratch() + [
+            pltpu.VMEM((128, D), BF16),
+            pltpu.VMEM((ROW, D), BF16),
+            pltpu.VMEM((D, ROW), BF16),
+            pltpu.VMEM((3, cols, ROW), BF16),
+            pltpu.SemaphoreType.DMA((3,)),
+        ],
         compiler_params=pltpu.CompilerParams(**PARAMS),
         cost_estimate=pl.CostEstimate(flops=2 * 10**10, bytes_accessed=10**7, transcendentals=0),
         name="attend_own",
@@ -340,13 +389,13 @@
         grid=(heads // GROUP, ROW // QB),
         in_specs=[whole(a.shape) for a in ins],
         out_specs=[
-            whole_out((3, cols, ROW)),
+            pl.BlockSpec(memory_space=pl.ANY),
             pl.BlockSpec((GROUP, ROW, QB), lambda h, q: (h, 0, q)),
             whole_out((cols, ROW)),
             whole_out((8, ROW)),
-            whole_out((ROW, D)),
-            whole_out((ROW, D)),
-            whole_out((D, ROW)),
+            pl.BlockSpec(memory_space=pl.ANY),
+            pl.BlockSpec(memory_space=pl.ANY),
+            pl.BlockSpec(memory_space=pl.ANY),
         ],
         out_shape=[
             sds((3, cols, ROW), BF16),
@@ -357,7 +406,13 @@
             sds((ROW, D), BF16),
             sds((D, ROW), BF16),
         ],
-        scratch_shapes=forward_scratch(),
+        scratch_shapes=forward_scratch() + [
+            pltpu.VMEM((3, cols, ROW), BF16),
+            pltpu.VMEM((ROW, D), F32),
+            pltpu.VMEM((ROW, D), BF16),
+            pltpu.VMEM((D, ROW), BF16),
+            pltpu.SemaphoreType.DMA((1 + 3 * (ROW // QB),)),
+        ],
         compiler_params=pltpu.CompilerParams(**PARAMS),
         cost_estimate=pl.CostEstimate(flops=2 * 10**10, bytes_accessed=10**7, transcendentals=0),
         name="attend_other",
@@ -378,7 +433,7 @@
     x_hbm, xt_hbm, og_hbm, mid_hbm, start_hbm, yt_hbm, qkv_own_hbm, qkv_oth_hbm,
     mix_own_hbm, mix_oth_hbm, inv_own_hbm, inv_oth_hbm, wq_own_hbm, wk_own_hbm, wv_own_hbm, wq_oth_hbm, wk_oth_hbm,
     wv_oth_hbm, wo_own_hbm, wo_oth_hbm,
-    result_ref, gtok_ref, out_in, out_out, out_q, out_k, out_v, out_o, out_small,
+    result_hbm, gtok_hbm, out_in, out_out, out_q, out_k, out_v, out_o, out_small,
     x, xt, og, mid, qkv, mix, inv, gmix, wqkv, wo, feed, gnf, dst, dqkv, kaug, vaug, doaug,
     tacc, gvec, gains, ptb, g, xsend, xrecv, ring, load_sem, late_sem, pt_sem, out_sem, xs_sem, xr_sem,
     send_sem, recv_sem,
@@ -425,9 +480,8 @@
     n_out = cols // 128
     n_chunks = 2 * n_ff + 4 * n_out + 1
     n_units = n_chunks
-    stages, n_halved, _ = plan_stages(n_rows)
-    n_stages = len(stages)
-    peers = stage_order(n_rows, 0)[2]
+    table, peers = stage_table(n_rows)
+    n_stages = len(table)
     core = {"heads": 1 - me}
 
     def swap(slot):
@@ -451,33 +505,24 @@
         swap(slot).wait()
         g[c] = (g[c].astype(F32) + xrecv[slot].astype(F32)).astype(BF16)
 
-    def stage_copy(k, c):
-        kind, j, n, slot = stages[k]
-        pick, peer, _ = stage_order(n_rows, c % 2)
-        base, size = 0, UNIT
-        for i in range(min(j, n_halved)):
-            size = size // 2
-            base = base + pick[i] * size
-        keep = base + pick[j] * n
-        give = base + (1 - pick[j]) * n
-        src, dst = {"halve": (give, keep), "swap": (base, base), "gather": (keep, give)}[kind]
-        src, dst = (pl.ds(pl.multiple_of(r, 16), n) for r in (src, dst))
-        par = c % SLOTS
+    def stage_copy(k, c, par, odd):
+        kind, n, slot, even_side, odd_side = table[k]
+        src, dst, peer = (p + odd * (q - p) for p, q in zip(even_side, odd_side))
         copy = pltpu.make_async_remote_copy(
-            src_ref=g.at[c, src, :],
+            src_ref=g.at[c, pl.ds(pl.multiple_of(src, 16), n), :],
             dst_ref=ring.at[par, slot : slot + n, :],
             send_sem=send_sem.at[k, par],
             recv_sem=recv_sem.at[k, par],
-            device_id={"rows": peer[j]},
+            device_id={"rows": peer},
             device_id_type=pl.DeviceIdType.MESH,
         )
-        return copy, dst
-
-    def stage_end(k, c):
-        kind, _, n, slot = stages[k]
-        copy, dst = stage_copy(k, c)
+        return copy, pl.ds(pl.multiple_of(dst, 16), n)
+
+    def stage_end(k, c, par, odd):
+        kind, n, slot = table[k][:3]
+        copy, dst = stage_copy(k, c, par, odd)
         copy.wait()
-        part = ring[c % SLOTS, slot : slot + n, :]
+        part = ring[par, slot : slot + n, :]
         if kind != "gather":
             part = (g[c, dst, :].astype(F32) + part.astype(F32)).astype(BF16)
         g[c, dst, :] = part
@@ -485,70 +530,73 @@
     def out_wait(par):
         pltpu.make_async_copy(g.at[0], out_in.at[:, 0:128], out_sem.at[par]).wait()
 
-    def out_start(c):
-        sem = out_sem.at[c % 2]
+    def out_start(c, odd):
+        sem = out_sem.at[odd]
 
         @pl.when(c >= 2)
         def _():
-            out_wait(c % 2)
+            out_wait(odd)
 
         def wide(ref, col):
             dst = ref.at[:, pl.ds(pl.multiple_of(col * 128, 128), 128)]
             pltpu.make_async_copy(g.at[c], dst, sem).start()
 
         def tall(ref, row):
-            for b in range(D // 128):
-                dst = ref.at[
-                    pl.ds(pl.multiple_of(row * 128, 128), 128), b * 128 : (b + 1) * 128
-                ]
-                pltpu.make_async_copy(g.at[c, b * 128 : (b + 1) * 128], dst, sem).start()
+            pltpu.make_async_copy(g.at[c], ref.at[row], sem).start()
 
         base = 2 * n_ff + n_out
 
-        @pl.when(jnp.logical_and(c < 2 * n_ff, c % 2 == 0))
+        @pl.when(jnp.logical_and(c < 2 * n_ff, odd == 0))
         def _():
             wide(out_in, c // 2)
 
-        @pl.when(jnp.logical_and(c < 2 * n_ff, c % 2 == 1))
+        @pl.when(jnp.logical_and(c < 2 * n_ff, odd == 1))
         def _():
             tall(out_out, c // 2)
 
-        @pl.when(jnp.logical_and(c >= 2 * n_ff, c < base))
+        @pl.when(c >= 2 * n_ff)
         def _():
-            tall(out_o, c - 2 * n_ff)
-
-        for m, ref in enumerate((out_q, out_k, out_v)):
-            at = jnp.logical_and(c >= base, c < n_chunks - 1)
-
-            @pl.when(jnp.logical_and(at, (c - base) % 3 == m))
+            @pl.when(c < base)
             def _():
-                wide(ref, (c - base) // 3)
-
-        @pl.when(c == n_chunks - 1)
-        def _():
-            tall(out_small, 0)
+                tall(out_o, c - 2 * n_ff)
+
+            for m, ref in enumerate((out_q, out_k, out_v)):
+                at = jnp.logical_and(c >= base, c < n_chunks - 1)
+
+                @pl.when(jnp.logical_and(at, (c - base) % 3 == m))
+                def _():
+                    wide(ref, (c - base) // 3)
+
+            @pl.when(c == n_chunks - 1)
+            def _():
+                tall(out_small, 0)
 
     wo_end = 2 * n_ff + n_out
     holes = ((wo_end, 2), (wo_end + 5, 1))
 
     def tick(t):
+        turn = lax.rem(t, SLOTS)
+        parity = lax.rem(t, 2)
         for k in range(n_stages, -1, -1):
             v = t - SPACING * k
             c = v
-            valid = v >= 0
+            live_unit = v >= 0
             for at, length in holes:
                 c = c - jnp.where(v >= at + length, length, 0)
-                valid = jnp.logical_and(valid, jnp.logical_or(v < at, v >= at + length))
-            valid = jnp.logical_and(valid, c < n_units)
-
-            @pl.when(valid)
-            def _():
+                live_unit = jnp.logical_and(live_unit, jnp.logical_or(v < at, v >= at + length))
+            par = turn + (-SPACING * k) % SLOTS
+            par = par - jnp.where(par >= SLOTS, SLOTS, 0)
+            odd = parity if SPACING * k % 2 == 0 else 1 - parity
+
+            def step(k=k, c=c, par=par, odd=odd):
                 if k > 0:
-                    stage_end(k - 1, c)
+                    stage_end(k - 1, c, par, odd)
                 if k < n_stages:
-                    stage_copy(k, c)[0].start()
-                if k == n_stages:
-                    out_start(c)
+                    stage_copy(k, c, par, odd)[0].start()
+                else:
+                    out_start(c, odd)
+
+            pl.when(jnp.logical_and(live_unit, c < n_units))(step)
 
     def collect_ff(e):
         for j in range(2):
@@ -574,10 +622,10 @@
                 barrier, inc=1, device_id=peer, device_id_type=pl.DeviceIdType.MESH
             )
         pl.semaphore_wait(barrier, len(peers) + 1)
+        feed[...] = jnp.zeros(feed.shape, F32)
+        gnf[...] = jnp.zeros(gnf.shape, F32)
         for copy in loads[:n_early]:
             copy.wait()
-        feed[...] = jnp.zeros(feed.shape, F32)
-        gnf[...] = jnp.zeros(gnf.shape, F32)
 
     @pl.when(s < n_ff)
     def _():
@@ -624,7 +672,9 @@
         t0 = 2 * (n_ff - 2)
         tick(t0)
         middle = mid[...]
-        result_ref[...] = (middle + feed[...]).astype(BF16)
+        dst[:, 0:D] = (middle + feed[...]).astype(BF16)
+        to_result = pltpu.make_async_copy(dst.at[:, 0:D], result_hbm, late_sem.at[2])
+        to_result.start()
         back, gain_grad = norm_back(middle, gain_f_ref[...][None, :], gnf[...])
         gmid = og[...].astype(F32) + back
         gains[0:1, :] = gain_grad
@@ -646,6 +696,8 @@
         kaug[DH:, :] = key_marks(own_row(seg_ref))
         vaug[DH:, :] = (iota((16, ROW), 0) < 3).astype(F32).astype(BF16)
         gvec[...] = jnp.zeros(gvec.shape, F32)
+        to_result.wait()
+        dst[...] = jnp.zeros(dst.shape, BF16)
         for copy in late:
             copy.wait()
         tick(t0 + 3)
@@ -675,28 +727,37 @@
         right = jnp.zeros((1, QB), F32)
         n_blocks = ROW // QB
 
+        def live(b):
+            ks = [
+                kb for kb in range(NBLK)
+                if max(kb * BT - (b + 1) * QB, b * QB - (kb + 1) * BT) + 1 < LONGEST
+            ]
+            return slice(ks[0] * BT, (ks[-1] + 1) * BT)
+
         def grad_probs(b):
-            return dot_tn(va, doaug[:, b * QB : (b + 1) * QB])
+            return dot_tn(va[:, live(b)], doaug[:, b * QB : (b + 1) * QB])
 
         dp = grad_probs(0)
         dqkv[2, out_rows, :] = dot_nt(dot_, pt_ref[...]).astype(BF16)
         for b in range(n_blocks):
             qs = slice(b * QB, (b + 1) * QB)
             ahead = grad_probs(b + 1) if b + 1 < n_blocks else None
-            ds = pt_ref[:, qs].astype(F32) * dp
+            ks = live(b)
+            ds = pt_ref[ks, qs].astype(F32) * dp
             for u in range(QB // BT):
                 qb = b * (QB // BT) + u
                 for d in (-1, 0, 1):
                     kb = qb + d
                     if 0 <= kb < NBLK:
+                        at = kb * BT - ks.start
                         tacc[:, 256 - 128 * d : 384 - 128 * d] += ds[
-                            kb * BT : (kb + 1) * BT, u * BT : (u + 1) * BT
+                            at : at + BT, u * BT : (u + 1) * BT
                         ]
-            dst[:, qs] = ds.astype(BF16)
+            dst[ks, qs] = ds.astype(BF16)
             dp = ahead
         for b in range(n_blocks):
             qs = slice(b * QB, (b + 1) * QB)
-            r = dot_nn(ka, dst[:, qs])
+            r = dot_nn(ka[:, live(b)], dst[live(b), qs])
             dqkv[0, out_rows, qs] = r[:DH].astype(BF16)
             sums = r[DH + 8 :]
             j = iota((8, QB), 0)
@@ -743,16 +804,17 @@
 
     def group_back(grp):
         for m in range(3):
-            grad = dqkv[m]
-            dw = dot_nt(xt[...], grad)
+            dw = dot_nt(xt[...], dqkv[m])
             emit(
-                (2 * n_ff + n_out + 3 * grp + m), group_slot(grp, m),
+                2 * n_ff + n_out + 3 * grp + m, group_slot(grp, m),
                 [dw[:, :128]], [dw[:, 128:]],
             )
-            cols_g = slice(grp * 128, (grp + 1) * 128)
+        cols_g = slice(grp * 128, (grp + 1) * 128)
+        for m in range(3):
             w = jnp.concatenate([wqkv[0, m, :, cols_g], wqkv[1, m, :, cols_g]], axis=1)
-            part = lax.dot_general(grad, w, (((0,), (1,)), ((), ())), preferred_element_type=F32)
-            gnf[...] += part
+            gnf[...] += lax.dot_general(
+                dqkv[m], w, (((0,), (1,)), ((), ())), preferred_element_type=F32
+            )
 
     for grp in range(n_heads // 4):
 
@@ -773,7 +835,9 @@
         picks = picks_t(seg)
         here = dot_tn(picks, (iota((128, 128), 0) < PROMPT).astype(F32).astype(BF16)) > 0.5
         for c in range(0, D, 128):
-            gtok_ref[:, c : c + 128] = jnp.where(here, 0.0, gstart[:, c : c + 128]).astype(BF16)
+            og[:, c : c + 128] = jnp.where(here, 0.0, gstart[:, c : c + 128]).astype(BF16)
+        to_gtok = pltpu.make_async_copy(og, gtok_hbm, late_sem.at[0])
+        to_gtok.start()
         high = gstart.astype(BF16)
         low = (gstart - high.astype(F32)).astype(BF16)
         tick(t0 + 1)
@@ -799,6 +863,7 @@
         def _(t):
             tick(t)
 
+        to_gtok.wait()
         out_wait(0)
         out_wait(1)
 
@@ -827,11 +892,11 @@
             whole(seg.shape), whole(gain_a.shape), whole(gain_f.shape),
             blk_in, blk_in, blk_out, blk_out,
         ] + [anyspec] * (2 + len(rest)),
-        out_specs=[whole((ROW, D)), whole((ROW, D))] + [anyspec] * 7,
+        out_specs=[anyspec] * 9,
         out_shape=[sds((ROW, D), BF16), sds((ROW, D), BF16)] + [
             sds(shape, BF16)
-            for shape in (win_own.shape, wout_own.shape)
-            + ((D, cols),) * 3 + ((cols, D), (128, D))
+            for shape in (win_own.shape, (n_ff, CH, 128))
+            + ((D, cols),) * 3 + ((cols // 128, CH, 128), (1, CH, 128))
         ],
         scratch_shapes=[
             pltpu.VMEM((ROW, D), BF16),
@@ -860,7 +925,7 @@
             pltpu.VMEM((8, CH, 128), BF16),
             pltpu.VMEM((SLOTS, ring_rows, 128), BF16),
             pltpu.SemaphoreType.DMA((18,)),
-            pltpu.SemaphoreType.DMA((2,)),
+            pltpu.SemaphoreType.DMA((3,)),
             pltpu.SemaphoreType.DMA((2,)),
             pltpu.SemaphoreType.DMA((2,)),
             pltpu.SemaphoreType.DMA((8,)),
@@ -875,18 +940,28 @@
     )(seg, gain_a, gain_f, win_own, win_oth, wout_own, wout_oth, pt_own, pt_oth, *rest)
 
 
+def untile(src, dst):
+    for c in range(src.shape[0]):
+        for b in range(D // 128):
+            dst[c * 128 : (c + 1) * 128, b * 128 : (b + 1) * 128] = src[
+                c, b * 128 : (b + 1) * 128, :
+            ].astype(F32)
+
+
 def finish(
     heads, result, gtok, small, g_q, g_k, g_v, g_wo, g_in, g_out,
     o_result, o_gtok, o_prompt, o_gain_a, o_q, o_k, o_v, o_wo, o_tab, o_gain_f, o_in, o_out, rows,
 ):
     o_result[...] = result[...]
     o_gtok[...] = gtok[...]
-    for src, dst in ((g_q, o_q), (g_k, o_k), (g_v, o_v), (g_wo, o_wo), (g_in, o_in), (g_out, o_out)):
+    for src, dst in ((g_q, o_q), (g_k, o_k), (g_v, o_v), (g_in, o_in)):
         dst[...] = src[...].astype(F32)
+    untile(g_out, o_out)
 
     @pl.when(pl.program_id(0) == 0)
     def _():
-        rows[...] = small[...].astype(F32)
+        untile(small, rows)
+        untile(g_wo, o_wo)
         o_prompt[...] = rows[0:PROMPT, :]
         o_gain_a[...] = rows[PROMPT, :]
         o_gain_f[...] = rows[PROMPT + 1, :]
@@ -897,27 +972,32 @@
             for k in range(heads)
         ]
         tab.append(jnp.zeros((8 - heads, 128), F32))
-        o_tab[...] = jnp.concatenate(tab, axis=0).T[0:NB, 0:heads]
+        o_tab[...] = jnp.concatenate(tab, axis=0)[0:heads, 0:NB]
 
 
 def run_finish(heads, result, gtok, small, *grads):
-    steps = 8
-
-    def part(a):
-        return pl.BlockSpec((a.shape[0] // steps, a.shape[1]), lambda i: (i, 0))
+    steps = 2
+
+    def part(shape):
+        zeros = (0,) * (len(shape) - 1)
+        return pl.BlockSpec((shape[0] // steps,) + shape[1:], lambda i: (i,) + zeros)
 
     g_q, g_k, g_v, g_wo, g_in, g_out = grads
+    wo_shape, out_shape = ((a.shape[0] * 128, D) for a in (g_wo, g_out))
     whole_1d = pl.BlockSpec((D,), lambda i: (0,))
     return pl.pallas_call(
         partial(finish, heads),
         grid=(steps,),
-        in_specs=[part(result), part(gtok), whole(small.shape)] + [part(a) for a in grads],
-        out_specs=[part(result), part(gtok), whole_out((PROMPT, D)), whole_1d]
-        + [part(a) for a in (g_q, g_k, g_v, g_wo)]
-        + [whole_out((NB, heads)), whole_1d, part(g_in), part(g_out)],
+        in_specs=[part(result.shape), part(gtok.shape), whole(small.shape)]
+        + [part(a.shape) for a in (g_q, g_k, g_v)]
+        + [whole(g_wo.shape), part(g_in.shape), part(g_out.shape)],
+        out_specs=[part(result.shape), part(gtok.shape), whole_out((PROMPT, D)), whole_1d]
+        + [part(a.shape) for a in (g_q, g_k, g_v)]
+        + [whole_out(wo_shape), whole_out((heads, NB)), whole_1d, part(g_in.shape), part(out_shape)],
         out_shape=[sds(result.shape, BF16), sds(gtok.shape, BF16), sds((PROMPT, D), F32), sds((D,), F32)]
-        + [sds(a.shape, F32) for a in (g_q, g_k, g_v, g_wo)]
-        + [sds((NB, heads), F32), sds((D,), F32), sds(g_in.shape, F32), sds(g_out.shape, F32)],
+        + [sds(a.shape, F32) for a in (g_q, g_k, g_v)]
+        + [sds(wo_shape, F32), sds((heads, NB), F32), sds((D,), F32)]
+        + [sds(g_in.shape, F32), sds(out_shape, F32)],
         scratch_shapes=[pltpu.VMEM((128, D), F32)],
         compiler_params=pltpu.CompilerParams(vmem_limit_bytes=62 * 1024 * 1024),
         name="finish",
@@ -934,11 +1014,11 @@
     def other(a):
         return lax.ppermute(a, "heads", swap)
 
-    tab_oth, wq_oth, wk_oth, wv_oth = (other(a) for a in (bias_table, w_query, w_key, w_value))
+    tab_oth, wq_oth, wk_oth, wv_oth = (other(a) for a in (bias_table.T, w_query, w_key, w_value))
     wo_oth, win_oth, wout_oth = other(w_attn_out), other(w_in), other(w_out)
     gain_a, gain_f = gain_attn, gain_ff
     start, yt, qkv_own, pt_own, mix_own, inv_own = run_first(
-        seg, tokens, prompt, gain_a, w_query, w_key, w_value, bias_table
+        seg, tokens, prompt, gain_a, w_query, w_key, w_value, bias_table.T
     )
     qkv_oth, pt_oth, mix_oth, inv_oth, middle, x, xt = run_second(
         seg, start, yt, gain_f, wq_oth, wk_oth, wv_oth, tab_oth, mix_own, w_attn_out, wo_oth
@@ -954,7 +1034,7 @@
         result, gtok, g_prompt, g_gain_a, g_q, g_k, g_v, g_wo, g_tab, g_gain_f, g_in, g_out,
     ) = run_finish(bias_table.shape[1], result, gtok, small, g_q, g_k, g_v, g_wo, g_in, g_out)
     return (
-        result, gtok, g_prompt, g_gain_a, g_q, g_k, g_v, g_wo, g_tab, g_gain_f, g_in, g_out,
+        result, gtok, g_prompt, g_gain_a, g_q, g_k, g_v, g_wo, g_tab.T, g_gain_f, g_in, g_out,
     )
 
 

time: 225 us -> 219 us (0.973)
  Pallas kernels: 220 us -> 215 us
  transfers between devices with their start and end apart: 7 -> 7, of which waited for: 1 -> 1; matrix products, arithmetic and copies ran while one was open for 0% -> 0% of each run, Pallas kernels for 18% -> 17%
where the time goes in v2:
time: 219 us; the launch traced here: 220 us
  Pallas kernels  215 us (98%)
    pallas_call x1, Pallas kernels, run_backward(): pl.pallas_call(partial(backward, n_ff, n_heads, n_rows), grid=(first + n_...  167 us
    pallas_call x1, Pallas kernels, run_second(): pl.pallas_call(forward_second, grid=(heads // GROUP, ROW // QB), in_specs...  20.8 us
    pallas_call x1, Pallas kernels, run_first(): pl.pallas_call(forward_first, grid=(heads // GROUP, ROW // QB), in_specs=...  17.7 us
    pallas_call x1, Pallas kernels, run_finish(): pl.pallas_call(partial(finish, heads), grid=(steps,), in_specs=[part(resu...  10 us
  transfers between devices with their start and end apart: 7, of which 1 were waited for; matrix products, arithmetic and copies ran while one was open for 0% of the time, Pallas kernels for 17%

profile of v2, /device:TPU:0, one launch (start us, length us, event | category | flops | bytes accessed | tf_op | source)
XLA Modules:
  0.0 220.1 jit_solution(11498830903644364039)
XLA Ops:
  0.6 0.5 collective-permute-start.2
  1.2 0.1 collective-permute-start.5
  1.2 0.4 collective-permute-start.3
  1.7 0.1 collective-permute-start.4
  1.8 0.4 collective-permute-start.6
  2.2 0.8 collective-permute-done.5.tab_ref
  3.0 0.4 collective-permute-start
  3.4 0.0 collective-permute-done.2.wq.wq_oth_hbm
  3.4 0.1 collective-permute-start.1
  3.5 17.7 %attend_own.1 = (bf16[1024,768]{1,0:T(8,128)(2,1)}, bf16[768,1024]{1,0:T(8,128)(2,1)}, bf16[3,384,1024]{2,1,0:T(8,128)(2,1)}, bf16[6,1024,1024]{2,1,0:T(8,128)(2...) custom-call(s32[2,1024]{1,0:T(2,128)} %seg_ref.5, bf16[1024,768]{1,0:T(8,128)(2,1)} %tok_ref.1, ...), custom_call_target="tpu_custom_call" | custom-call | flops 20000000000 | bytes 10000000 | tf_op jit(solution)/shard_map/attend_own/pallas_call | solution.py:350
  21.2 0.0 copy-done.4
  21.2 0.0 collective-permute-done.3.wk.wk_oth_hbm
  21.2 0.0 copy-start.1
  21.2 0.0 collective-permute-done.4.wv.wv_oth_hbm
  21.3 0.0 collective-permute-done.6.wo_oth.wo_oth_hbm
  21.3 0.0 copy-start.3
  21.3 0.8 copy-done.1
  22.0 0.2 copy-done.2
  22.3 0.2 copy-done.3
  22.4 20.8 %attend_other.1 = (bf16[3,384,1024]{2,1,0:T(8,128)(2,1)}, bf16[6,1024,1024]{2,1,0:T(8,128)(2,1)}, bf16[384,1024]{1,0:T(8,128)(2,1)}, f32[8,1024]{1,0:T(8,128)}, ...) custom-call(s32[2,1024]{1,0:T(2,128)} %seg_ref.5, ...), custom_call_target="tpu_custom_call" | custom-call | flops 20000000000 | bytes 10000000 | tf_op jit(solution)/shard_map/attend_other/pallas_call | solution.py:387
  43.2 0.0 collective-permute-done.win_oth
  43.3 0.0 collective-permute-done.1.wout_oth
  43.3 166.5 %backward.1 = (bf16[1024,768]{1,0:T(8,128)(2,1)}, bf16[1024,768]{1,0:T(8,128)(2,1)}, bf16[768,1536]{1,0:T(8,128)(2,1)}, bf16[12,768,128]{2,1,0:T(8,128)(2,1)}, b...) custom-call(s32[2,1024]{1,0:T(2,128)} %seg_ref.5, ...), custom_call_target="tpu_custom_call" | custom-call | tf_op jit(solution)/shard_map/backward/pallas_call | solution.py:888
  209.8 10.0 %finish.1 = (bf16[1024,768]{1,0:T(8,128)(2,1)}, bf16[1024,768]{1,0:T(8,128)(2,1)}, f32[100,768]{1,0:T(8,128)}, f32[768]{0:T(1024)}, f32[768,384]{1,0:T(8,128)}, ...) custom-call(bf16[1024,768]{1,0:T(8,128)(2,1)} %get-tuple-element.59., ...), custom_call_target="tpu_custom_call" | custom-call | tf_op jit(solution)/shard_map/finish/pallas_call | solution.py:988
  (4 shorter events, 0.0 us)
Async XLA Ops:
  0.6 2.7 %collective-permute-start.2 = (bf16[768,384]{1,0:T(8,128)(2,1)}, bf16[768,384]{1,0:T(8,128)(2,1)S(1)}, u32[]{:S(2)}, u32[]{:S(2)}) collective-permute-start(bf16[768,384]{1,0:T(8,128)(2,1)} %wq_own_hbm.1), channel_id=1, source_target_pairs={{0,1},{1,0},{2,3},{3,2},{4,5},{5,4},{6,7},{7,6},{8,9},{9,8},{10,11... | collective-permute-start | bytes 1769480 | tf_op jit(solution)/shard_map/ppermute | solution.py:1015
  1.2 1.8 collective-permute-start.5
  1.2 20.0 %collective-permute-start.3 = (bf16[768,384]{1,0:T(8,128)(2,1)}, bf16[768,384]{1,0:T(8,128)(2,1)S(1)}, u32[]{:S(2)}, u32[]{:S(2)}) collective-permute-start(bf16[768,384]{1,0:T(8,128)(2,1)} %wk_own_hbm.1), channel_id=1, source_target_pairs={{0,1},{1,0},{2,3},{3,2},{4,5},{5,4},{6,7},{7,6},{8,9},{9,8},{10,11... | collective-permute-start | bytes 1769480 | tf_op jit(solution)/shard_map/ppermute | solution.py:1015
  1.7 19.6 %collective-permute-start.4 = (bf16[768,384]{1,0:T(8,128)(2,1)}, bf16[768,384]{1,0:T(8,128)(2,1)S(1)}, u32[]{:S(2)}, u32[]{:S(2)}) collective-permute-start(bf16[768,384]{1,0:T(8,128)(2,1)} %wv_own_hbm.1), channel_id=1, source_target_pairs={{0,1},{1,0},{2,3},{3,2},{4,5},{5,4},{6,7},{7,6},{8,9},{9,8},{10,11... | collective-permute-start | bytes 1769480 | tf_op jit(solution)/shard_map/ppermute | solution.py:1015
  1.8 19.5 %collective-permute-start.6 = (bf16[384,768]{1,0:T(8,128)(2,1)}, bf16[384,768]{1,0:T(8,128)(2,1)S(1)}, u32[]{:S(2)}, u32[]{:S(2)}) collective-permute-start(bf16[384,768]{1,0:T(8,128)(2,1)} %wo_own_hbm.1), channel_id=1, source_target_pairs={{0,1},{1,0},{2,3},{3,2},{4,5},{5,4},{6,7},{7,6},{8,9},{9,8},{10,11... | collective-permute-start | bytes 1769480 | tf_op jit(solution)/shard_map/ppermute | solution.py:1015
  3.0 18.2 %copy-start.4 = (bf16[6,32]{1,0:T(8,128)(2,1)}, bf16[6,32]{1,0:T(8,128)(2,1)S(1)}, u32[]{:S(2)}) copy-start(bf16[6,32]{1,0:T(8,128)(2,1)S(1)} %collective-permute-done.5.tab_ref) | copy-start | bytes 1156
  3.0 40.2 %collective-permute-start = (bf16[768,1536]{1,0:T(8,128)(2,1)}, bf16[768,1536]{1,0:T(8,128)(2,1)}, u32[]{:S(2)}, u32[]{:S(2)}) collective-permute-start(bf16[768,1536]{1,0:T(8,128)(2,1)} %win_own.1), channel_id=1, source_target_pairs={{0,1},{1,0},{2,3},{3,2},{4,5},{5,4},{6,7},{7,6},{8,9},{9,8},{10,11... | collective-permute-start | bytes 7077896 | tf_op jit(solution)/shard_map/ppermute | solution.py:1015
  3.4 17.8 %copy-start = (bf16[768,384]{1,0:T(8,128)(2,1)}, bf16[768,384]{1,0:T(8,128)(2,1)S(1)}, u32[]{:S(2)}) copy-start(bf16[768,384]{1,0:T(8,128)(2,1)S(1)} %collective-permute-done.2.wq.wq_oth_hbm) | copy-start | bytes 1769476
  3.4 39.9 %collective-permute-start.1 = (bf16[1536,768]{1,0:T(8,128)(2,1)}, bf16[1536,768]{1,0:T(8,128)(2,1)}, u32[]{:S(2)}, u32[]{:S(2)}) collective-permute-start(bf16[1536,768]{1,0:T(8,128)(2,1)} %wout_own.1), channel_id=1, source_target_pairs={{0,1},{1,0},{2,3},{3,2},{4,5},{5,4},{6,7},{7,6},{8,9},{9,8},{10,11... | collective-permute-start | bytes 7077896 | tf_op jit(solution)/shard_map/ppermute | solution.py:1015
  21.2 0.8 copy-start.1
  21.2 1.0 copy-start.2
  21.3 1.2 copy-start.3

commit v3 on v2

--- a/solution.py
+++ b/solution.py
@@ -181,8 +181,11 @@
 def forward_first(
     seg_ref, tok_ref, prompt_ref, gain_ref, wq, wk, wv, tab_ref,
     start_ref, yt_ref, qkv_ref, pt_ref, mixed_ref, inv_ref,
-    table_f, span, kaug, qaug, vaug, kn, strip, padded, start_s, yt_s, qkv_s, sem,
+    table_f, span, kaug, qaug, vaug, kn, strip, padded, start_s, yt_s, qkv_s, sem, w_s, w_sem,
 ):
+    loads = [
+        pltpu.make_async_copy(w, w_s.at[m], w_sem.at[m]) for m, w in enumerate((wq, wk, wv))
+    ]
     copies = [
         pltpu.make_async_copy(a, b, sem.at[k])
         for k, (a, b) in enumerate(((start_s, start_ref), (yt_s, yt_ref), (qkv_s, qkv_ref)))
@@ -193,6 +196,8 @@
 
     @pl.when(first)
     def _():
+        for copy in loads:
+            copy.start()
         padded[...] = jnp.zeros(padded.shape, BF16)
         padded[0:PROMPT, :] = prompt_ref[...]
         picks = picks_t(seg)
@@ -212,7 +217,9 @@
         yt = (start * inv * gain_ref[...][None, :]).astype(BF16).T
         yt_s[...] = yt
         copies[1].start()
-        project_t((wq, wk, wv), yt, qkv_s)
+        for copy in loads:
+            copy.wait()
+        project_t([w_s.at[m] for m in range(3)], yt, qkv_s)
         copies[2].start()
         head_setup(seg, tab_ref, table_f, span, kaug, qaug, vaug, strip)
 
@@ -230,7 +237,14 @@
     seg_ref, start_ref, yt_ref, gain_ref, wq, wk, wv, tab_ref, mixed_own, wo_own, wo_oth,
     qkv_ref, pt_ref, mixed_ref, inv_ref, middle_ref, x_ref, xt_ref,
     table_f, span, kaug, qaug, vaug, kn, strip, qkv_s, middle_s, x_s, xt_s, sem,
+    w_s, yt_s, start_s, mixed_s, wo_s, w_sem,
 ):
+    pairs = [(w, w_s.at[m]) for m, w in enumerate((wq, wk, wv))]
+    pairs += [
+        (yt_ref, yt_s), (start_ref, start_s), (mixed_own, mixed_s), (wo_own, wo_s.at[0]),
+        (wo_oth, wo_s.at[1]),
+    ]
+    loads = [pltpu.make_async_copy(a, b, w_sem.at[k]) for k, (a, b) in enumerate(pairs)]
     qkv_copy = pltpu.make_async_copy(qkv_s, qkv_ref, sem.at[0])
     step, q = pl.program_id(0), pl.program_id(1)
     first = jnp.logical_and(step == 0, q == 0)
@@ -238,9 +252,13 @@
 
     @pl.when(first)
     def _():
-        project_t((wq, wk, wv), yt_ref[...], qkv_s)
+        for copy in loads:
+            copy.start()
+        head_setup(seg, tab_ref, table_f, span, kaug, qaug, vaug, strip)
+        for copy in loads[:4]:
+            copy.wait()
+        project_t([w_s.at[m] for m in range(3)], yt_s[...], qkv_s)
         qkv_copy.start()
-        head_setup(seg, tab_ref, table_f, span, kaug, qaug, vaug, strip)
 
     attend_heads(
         step, q, seg, table_f, span, qkv_s, kaug, qaug, vaug, kn, strip, pt_ref, mixed_ref, inv_ref
@@ -248,11 +266,13 @@
 
     @pl.when(jnp.logical_and(step == pl.num_programs(0) - 1, q == pl.num_programs(1) - 1))
     def _():
+        for copy in loads[4:]:
+            copy.wait()
         copies = []
         for k in range(0, ROW, QB):
             r = slice(k, k + QB)
-            attn = dot_tn(mixed_own[:, r], wo_own[...]) + dot_tn(mixed_ref[:, r], wo_oth[...])
-            middle = start_ref[r, :].astype(F32) + attn
+            attn = dot_tn(mixed_s[:, r], wo_s[0]) + dot_tn(mixed_ref[:, r], wo_s[1])
+            middle = start_s[r, :].astype(F32) + attn
             middle_s[r, :] = middle
             inv = lax.rsqrt(jnp.mean(middle * middle, axis=1, keepdims=True) + EPS)
             x = (middle * inv * gain_ref[...][None, :]).astype(BF16)
@@ -350,7 +370,9 @@
     return pl.pallas_call(
         forward_first,
         grid=(heads // GROUP, ROW // QB),
-        in_specs=[whole(a.shape) for a in (seg, tok, prompt, gain, wq, wk, wv, tab)],
+        in_specs=[whole(a.shape) for a in (seg, tok, prompt, gain)]
+        + [pl.BlockSpec(memory_space=pl.ANY)] * 3
+        + [whole(tab.shape)],
         out_specs=[
             pl.BlockSpec(memory_space=pl.ANY),
             pl.BlockSpec(memory_space=pl.ANY),
@@ -373,6 +395,8 @@
             pltpu.VMEM((D, ROW), BF16),
             pltpu.VMEM((3, cols, ROW), BF16),
             pltpu.SemaphoreType.DMA((3,)),
+            pltpu.VMEM((3, D, cols), BF16),
+            pltpu.SemaphoreType.DMA((3,)),
         ],
         compiler_params=pltpu.CompilerParams(**PARAMS),
         cost_estimate=pl.CostEstimate(flops=2 * 10**10, bytes_accessed=10**7, transcendentals=0),
@@ -387,7 +411,10 @@
     return pl.pallas_call(
         forward_second,
         grid=(heads // GROUP, ROW // QB),
-        in_specs=[whole(a.shape) for a in ins],
+        in_specs=[
+            whole(a.shape) if a is seg or a is gain or a is tab else pl.BlockSpec(memory_space=pl.ANY)
+            for a in ins
+        ],
         out_specs=[
             pl.BlockSpec(memory_space=pl.ANY),
             pl.BlockSpec((GROUP, ROW, QB), lambda h, q: (h, 0, q)),
@@ -412,6 +439,12 @@
             pltpu.VMEM((ROW, D), BF16),
             pltpu.VMEM((D, ROW), BF16),
             pltpu.SemaphoreType.DMA((1 + 3 * (ROW // QB),)),
+            pltpu.VMEM((3, D, cols), BF16),
+            pltpu.VMEM((D, ROW), BF16),
+            pltpu.VMEM((ROW, D), BF16),
+            pltpu.VMEM((cols, ROW), BF16),
+            pltpu.VMEM((2, cols, D), BF16),
+            pltpu.SemaphoreType.DMA((8,)),
         ],
         compiler_params=pltpu.CompilerParams(**PARAMS),
         cost_estimate=pl.CostEstimate(flops=2 * 10**10, bytes_accessed=10**7, transcendentals=0),
@@ -646,10 +679,10 @@
         active = jnp.concatenate(acts, axis=0)
         gpre = jnp.concatenate(gpres, axis=0)
 
-        @pl.when(s >= 2)
+        @pl.when(s >= 1)
         def _():
-            collect_ff(s - 2)
-            tick(2 * (s - 2))
+            collect_ff(s - 1)
+            tick(2 * (s - 1))
 
         dwin = dot_nn(xt[...], gpre)
         dwout = dot_tn(active, og[...])
@@ -657,9 +690,9 @@
         emit(2 * s, 2 * (s % 4), [dwin[:, :FFC]], [dwin[:, FFC:]])
         emit(2 * s + 1, 2 * (s % 4) + 1, lanes(dwout[:FFC]), lanes(dwout[FFC:]))
 
-        @pl.when(s >= 2)
+        @pl.when(s >= 1)
         def _():
-            tick(2 * (s - 2) + 1)
+            tick(2 * (s - 1) + 1)
 
     @pl.when(s == n_ff)
     def _():
@@ -668,9 +701,7 @@
         pt_start(0)
         for copy in loads[n_early:]:
             copy.wait()
-        collect_ff(n_ff - 2)
         t0 = 2 * (n_ff - 2)
-        tick(t0)
         middle = mid[...]
         dst[:, 0:D] = (middle + feed[...]).astype(BF16)
         to_result = pltpu.make_async_copy(dst.at[:, 0:D], result_hbm, late_sem.at[2])
@@ -679,7 +710,6 @@
         gmid = og[...].astype(F32) + back
         gains[0:1, :] = gain_grad
         mid[...] = gmid
-        tick(t0 + 1)
         ga = gmid.astype(BF16)
         dwo = [dot_nn(mix[o], ga) for o in range(2)]
         collect_ff(n_ff - 1)

time: 219 us -> 215 us (0.982)
  Pallas kernels: 215 us -> 211 us
    pallas_call x1, Pallas kernels: 167 us -> 163 us  [run_backward(): pl.pallas_call(partial(backward, n_ff, n_heads, n_rows), grid=(first + n_...]
  transfers between devices with their start and end apart: 7 -> 7, of which waited for: 1 -> 1; matrix products, arithmetic and copies ran while one was open for 0% -> 0% of each run, Pallas kernels for 17% -> 18%
where the time goes in v3:
time: 215 us; the launch traced here: 216 us
  Pallas kernels  211 us (98%)
    pallas_call x1, Pallas kernels, run_backward(): pl.pallas_call(partial(backward, n_ff, n_heads, n_rows), grid=(first + n_...  163 us
    pallas_call x1, Pallas kernels, run_second(): pl.pallas_call(forward_second, grid=(heads // GROUP, ROW // QB), in_specs...  20.9 us
    pallas_call x1, Pallas kernels, run_first(): pl.pallas_call(forward_first, grid=(heads // GROUP, ROW // QB), in_specs=...  17.4 us
    pallas_call x1, Pallas kernels, run_finish(): pl.pallas_call(partial(finish, heads), grid=(steps,), in_specs=[part(resu...  10 us
  transfers between devices with their start and end apart: 7, of which 1 were waited for; matrix products, arithmetic and copies ran while one was open for 0% of the time, Pallas kernels for 18%

profile of v3, /device:TPU:0, one launch (start us, length us, event | category | flops | bytes accessed | tf_op | source)
XLA Modules:
  0.0 216.3 jit_solution(360087897377613254)
XLA Ops:
  0.6 0.5 collective-permute-start.2
  1.2 0.1 collective-permute-start.5
  1.2 0.4 collective-permute-start.3
  1.7 0.1 collective-permute-start.4
  1.8 0.4 collective-permute-start.6
  2.2 0.8 collective-permute-done.5.tab_ref
  3.0 0.4 collective-permute-start
  3.4 0.0 collective-permute-done.2.wq.wq_oth_hbm
  3.4 0.1 collective-permute-start.1
  3.5 17.4 %attend_own.1 = (bf16[1024,768]{1,0:T(8,128)(2,1)}, bf16[768,1024]{1,0:T(8,128)(2,1)}, bf16[3,384,1024]{2,1,0:T(8,128)(2,1)}, bf16[6,1024,1024]{2,1,0:T(8,128)(2...) custom-call(s32[2,1024]{1,0:T(2,128)} %seg_ref.5, bf16[1024,768]{1,0:T(8,128)(2,1)} %tok_ref.1, ...), custom_call_target="tpu_custom_call" | custom-call | flops 20000000000 | bytes 10000000 | tf_op jit(solution)/shard_map/attend_own/pallas_call | solution.py:370
  20.9 0.0 copy-done.4
  21.0 0.0 collective-permute-done.3.wk.wk_oth_hbm
  21.0 0.0 copy-start.1
  21.0 0.0 collective-permute-done.4.wv.wv_oth_hbm
  21.0 0.0 collective-permute-done.6.wo_oth.wo_oth_hbm
  21.0 0.0 copy-start.3
  21.0 0.8 copy-done.1
  21.8 0.2 copy-done.2
  22.0 0.2 copy-done.3
  22.2 20.9 %attend_other.1 = (bf16[3,384,1024]{2,1,0:T(8,128)(2,1)}, bf16[6,1024,1024]{2,1,0:T(8,128)(2,1)}, bf16[384,1024]{1,0:T(8,128)(2,1)}, f32[8,1024]{1,0:T(8,128)}, ...) custom-call(s32[2,1024]{1,0:T(2,128)} %seg_ref.5, ...), custom_call_target="tpu_custom_call" | custom-call | flops 20000000000 | bytes 10000000 | tf_op jit(solution)/shard_map/attend_other/pallas_call | solution.py:411
  43.1 0.0 collective-permute-done.win_oth
  43.1 0.0 collective-permute-done.1.wout_oth
  43.1 162.9 %backward.1 = (bf16[1024,768]{1,0:T(8,128)(2,1)}, bf16[1024,768]{1,0:T(8,128)(2,1)}, bf16[768,1536]{1,0:T(8,128)(2,1)}, bf16[12,768,128]{2,1,0:T(8,128)(2,1)}, b...) custom-call(s32[2,1024]{1,0:T(2,128)} %seg_ref.5, ...), custom_call_target="tpu_custom_call" | custom-call | tf_op jit(solution)/shard_map/backward/pallas_call | solution.py:918
  206.0 10.0 %finish.1 = (bf16[1024,768]{1,0:T(8,128)(2,1)}, bf16[1024,768]{1,0:T(8,128)(2,1)}, f32[100,768]{1,0:T(8,128)}, f32[768]{0:T(1024)}, f32[768,384]{1,0:T(8,128)}, ...) custom-call(bf16[1024,768]{1,0:T(8,128)(2,1)} %get-tuple-element.59., ...), custom_call_target="tpu_custom_call" | custom-call | tf_op jit(solution)/shard_map/finish/pallas_call | solution.py:1018
  (4 shorter events, 0.0 us)
Async XLA Ops:
  0.6 2.7 %collective-permute-start.2 = (bf16[768,384]{1,0:T(8,128)(2,1)}, bf16[768,384]{1,0:T(8,128)(2,1)S(1)}, u32[]{:S(2)}, u32[]{:S(2)}) collective-permute-start(bf16[768,384]{1,0:T(8,128)(2,1)} %wq_own_hbm.1), channel_id=1, source_target_pairs={{0,1},{1,0},{2,3},{3,2},{4,5},{5,4},{6,7},{7,6},{8,9},{9,8},{10,11... | collective-permute-start | bytes 1769480 | tf_op jit(solution)/shard_map/ppermute | solution.py:1045
  1.2 1.8 collective-permute-start.5
  1.2 19.7 %collective-permute-start.3 = (bf16[768,384]{1,0:T(8,128)(2,1)}, bf16[768,384]{1,0:T(8,128)(2,1)S(1)}, u32[]{:S(2)}, u32[]{:S(2)}) collective-permute-start(bf16[768,384]{1,0:T(8,128)(2,1)} %wk_own_hbm.1), channel_id=1, source_target_pairs={{0,1},{1,0},{2,3},{3,2},{4,5},{5,4},{6,7},{7,6},{8,9},{9,8},{10,11... | collective-permute-start | bytes 1769480 | tf_op jit(solution)/shard_map/ppermute | solution.py:1045
  1.7 19.3 %collective-permute-start.4 = (bf16[768,384]{1,0:T(8,128)(2,1)}, bf16[768,384]{1,0:T(8,128)(2,1)S(1)}, u32[]{:S(2)}, u32[]{:S(2)}) collective-permute-start(bf16[768,384]{1,0:T(8,128)(2,1)} %wv_own_hbm.1), channel_id=1, source_target_pairs={{0,1},{1,0},{2,3},{3,2},{4,5},{5,4},{6,7},{7,6},{8,9},{9,8},{10,11... | collective-permute-start | bytes 1769480 | tf_op jit(solution)/shard_map/ppermute | solution.py:1045
  1.8 19.3 %collective-permute-start.6 = (bf16[384,768]{1,0:T(8,128)(2,1)}, bf16[384,768]{1,0:T(8,128)(2,1)S(1)}, u32[]{:S(2)}, u32[]{:S(2)}) collective-permute-start(bf16[384,768]{1,0:T(8,128)(2,1)} %wo_own_hbm.1), channel_id=1, source_target_pairs={{0,1},{1,0},{2,3},{3,2},{4,5},{5,4},{6,7},{7,6},{8,9},{9,8},{10,11... | collective-permute-start | bytes 1769480 | tf_op jit(solution)/shard_map/ppermute | solution.py:1045
  3.0 17.9 %copy-start.4 = (bf16[6,32]{1,0:T(8,128)(2,1)}, bf16[6,32]{1,0:T(8,128)(2,1)S(1)}, u32[]{:S(2)}) copy-start(bf16[6,32]{1,0:T(8,128)(2,1)S(1)} %collective-permute-done.5.tab_ref) | copy-start | bytes 1156
  3.0 40.1 %collective-permute-start = (bf16[768,1536]{1,0:T(8,128)(2,1)}, bf16[768,1536]{1,0:T(8,128)(2,1)}, u32[]{:S(2)}, u32[]{:S(2)}) collective-permute-start(bf16[768,1536]{1,0:T(8,128)(2,1)} %win_own.1), channel_id=1, source_target_pairs={{0,1},{1,0},{2,3},{3,2},{4,5},{5,4},{6,7},{7,6},{8,9},{9,8},{10,11... | collective-permute-start | bytes 7077896 | tf_op jit(solution)/shard_map/ppermute | solution.py:1045
  3.4 17.6 %copy-start = (bf16[768,384]{1,0:T(8,128)(2,1)}, bf16[768,384]{1,0:T(8,128)(2,1)S(1)}, u32[]{:S(2)}) copy-start(bf16[768,384]{1,0:T(8,128)(2,1)S(1)} %collective-permute-done.2.wq.wq_oth_hbm) | copy-start | bytes 1769476
  3.4 39.7 %collective-permute-start.1 = (bf16[1536,768]{1,0:T(8,128)(2,1)}, bf16[1536,768]{1,0:T(8,128)(2,1)}, u32[]{:S(2)}, u32[]{:S(2)}) collective-permute-start(bf16[1536,768]{1,0:T(8,128)(2,1)} %wout_own.1), channel_id=1, source_target_pairs={{0,1},{1,0},{2,3},{3,2},{4,5},{5,4},{6,7},{7,6},{8,9},{9,8},{10,11... | collective-permute-start | bytes 7077896 | tf_op jit(solution)/shard_map/ppermute | solution.py:1045
  21.0 0.8 copy-start.1
  21.0 1.0 copy-start.2
  21.0 1.2 copy-start.3

commit v4 on v3

--- a/solution.py
+++ b/solution.py
@@ -28,7 +28,7 @@
 GROUP = 3
 SIZES = (2, 3, 4, 5, 6, 8)
 SPACING = 3
-SLOTS = 8
+SLOTS = 9
 BT = 128
 NBLK = ROW // BT
 
@@ -605,7 +605,7 @@
                 tall(out_small, 0)
 
     wo_end = 2 * n_ff + n_out
-    holes = ((wo_end, 2), (wo_end + 5, 1))
+    holes = ((wo_end, 3), (wo_end + 6, 2))
 
     def tick(t):
         turn = lax.rem(t, SLOTS)
@@ -830,7 +830,7 @@
             def _():
                 collect_group(e)
 
-        tick(2 * n_ff + i)
+        tick(2 * n_ff + i + i // 4)
 
     def group_back(grp):
         for m in range(3):
@@ -845,6 +845,8 @@
             gnf[...] += lax.dot_general(
                 dqkv[m], w, (((0,), (1,)), ((), ())), preferred_element_type=F32
             )
+        if grp < 2:
+            tick(2 * n_ff + 5 * grp + 4)
 
     for grp in range(n_heads // 4):
 
@@ -860,7 +862,7 @@
         gstart = mid[...] + back
         n_groups = n_heads // 4
         collect_group(n_groups - 1)
-        t0 = 2 * n_ff + n_heads
+        t0 = 2 * n_ff + n_heads + 2
         tick(t0)
         picks = picks_t(seg)
         here = dot_tn(picks, (iota((128, 128), 0) < PROMPT).astype(F32).astype(BF16)) > 0.5

time: 215 us -> 214 us (level)
  no operation moved by 1% of the time
where the time goes in v4:
time: 214 us; the launch traced here: 215 us
  Pallas kernels  210 us (98%)
    pallas_call x1, Pallas kernels, run_backward(): pl.pallas_call(partial(backward, n_ff, n_heads, n_rows), grid=(first + n_...  162 us
    pallas_call x1, Pallas kernels, run_second(): pl.pallas_call(forward_second, grid=(heads // GROUP, ROW // QB), in_specs...  20.9 us
    pallas_call x1, Pallas kernels, run_first(): pl.pallas_call(forward_first, grid=(heads // GROUP, ROW // QB), in_specs=...  17.4 us
    pallas_call x1, Pallas kernels, run_finish(): pl.pallas_call(partial(finish, heads), grid=(steps,), in_specs=[part(resu...  10 us
  transfers between devices with their start and end apart: 7, of which 1 were waited for; matrix products, arithmetic and copies ran while one was open for 0% of the time, Pallas kernels for 18%

profile of v4, /device:TPU:0, one launch (start us, length us, event | category | flops | bytes accessed | tf_op | source)
XLA Modules:
  0.0 215.1 jit_solution(13101218939364349718)
XLA Ops:
  0.6 0.5 collective-permute-start.2
  1.2 0.1 collective-permute-start.5
  1.2 0.4 collective-permute-start.3
  1.7 0.1 collective-permute-start.4
  1.8 0.4 collective-permute-start.6
  2.2 0.8 collective-permute-done.5.tab_ref
  3.0 0.4 collective-permute-start
  3.4 0.0 collective-permute-done.2.wq.wq_oth_hbm
  3.4 0.1 collective-permute-start.1
  3.5 17.4 %attend_own.1 = (bf16[1024,768]{1,0:T(8,128)(2,1)}, bf16[768,1024]{1,0:T(8,128)(2,1)}, bf16[3,384,1024]{2,1,0:T(8,128)(2,1)}, bf16[6,1024,1024]{2,1,0:T(8,128)(2...) custom-call(s32[2,1024]{1,0:T(2,128)} %seg_ref.5, bf16[1024,768]{1,0:T(8,128)(2,1)} %tok_ref.1, ...), custom_call_target="tpu_custom_call" | custom-call | flops 20000000000 | bytes 10000000 | tf_op jit(solution)/shard_map/attend_own/pallas_call | solution.py:370
  20.9 0.0 copy-done.4
  20.9 0.0 copy-done
  21.0 0.0 collective-permute-done.3.wk.wk_oth_hbm
  21.0 0.0 copy-start.1
  21.0 0.0 collective-permute-done.4.wv.wv_oth_hbm
  21.0 0.0 collective-permute-done.6.wo_oth.wo_oth_hbm
  21.0 0.8 copy-done.1
  21.8 0.2 copy-done.2
  22.0 0.2 copy-done.3
  22.2 20.9 %attend_other.1 = (bf16[3,384,1024]{2,1,0:T(8,128)(2,1)}, bf16[6,1024,1024]{2,1,0:T(8,128)(2,1)}, bf16[384,1024]{1,0:T(8,128)(2,1)}, f32[8,1024]{1,0:T(8,128)}, ...) custom-call(s32[2,1024]{1,0:T(2,128)} %seg_ref.5, ...), custom_call_target="tpu_custom_call" | custom-call | flops 20000000000 | bytes 10000000 | tf_op jit(solution)/shard_map/attend_other/pallas_call | solution.py:411
  43.1 0.0 collective-permute-done.win_oth
  43.1 0.0 collective-permute-done.1.wout_oth
  43.1 161.7 %backward.1 = (bf16[1024,768]{1,0:T(8,128)(2,1)}, bf16[1024,768]{1,0:T(8,128)(2,1)}, bf16[768,1536]{1,0:T(8,128)(2,1)}, bf16[12,768,128]{2,1,0:T(8,128)(2,1)}, b...) custom-call(s32[2,1024]{1,0:T(2,128)} %seg_ref.5, ...), custom_call_target="tpu_custom_call" | custom-call | tf_op jit(solution)/shard_map/backward/pallas_call | solution.py:920
  204.8 10.0 %finish.1 = (bf16[1024,768]{1,0:T(8,128)(2,1)}, bf16[1024,768]{1,0:T(8,128)(2,1)}, f32[100,768]{1,0:T(8,128)}, f32[768]{0:T(1024)}, f32[768,384]{1,0:T(8,128)}, ...) custom-call(bf16[1024,768]{1,0:T(8,128)(2,1)} %get-tuple-element.59., ...), custom_call_target="tpu_custom_call" | custom-call | tf_op jit(solution)/shard_map/finish/pallas_call | solution.py:1020
  (4 shorter events, 0.0 us)
Async XLA Ops:
  0.6 2.7 %collective-permute-start.2 = (bf16[768,384]{1,0:T(8,128)(2,1)}, bf16[768,384]{1,0:T(8,128)(2,1)S(1)}, u32[]{:S(2)}, u32[]{:S(2)}) collective-permute-start(bf16[768,384]{1,0:T(8,128)(2,1)} %wq_own_hbm.1), channel_id=1, source_target_pairs={{0,1},{1,0},{2,3},{3,2},{4,5},{5,4},{6,7},{7,6},{8,9},{9,8},{10,11... | collective-permute-start | bytes 1769480 | tf_op jit(solution)/shard_map/ppermute | solution.py:1047
  1.2 1.8 collective-permute-start.5
  1.2 19.7 %collective-permute-start.3 = (bf16[768,384]{1,0:T(8,128)(2,1)}, bf16[768,384]{1,0:T(8,128)(2,1)S(1)}, u32[]{:S(2)}, u32[]{:S(2)}) collective-permute-start(bf16[768,384]{1,0:T(8,128)(2,1)} %wk_own_hbm.1), channel_id=1, source_target_pairs={{0,1},{1,0},{2,3},{3,2},{4,5},{5,4},{6,7},{7,6},{8,9},{9,8},{10,11... | collective-permute-start | bytes 1769480 | tf_op jit(solution)/shard_map/ppermute | solution.py:1047
  1.7 19.3 %collective-permute-start.4 = (bf16[768,384]{1,0:T(8,128)(2,1)}, bf16[768,384]{1,0:T(8,128)(2,1)S(1)}, u32[]{:S(2)}, u32[]{:S(2)}) collective-permute-start(bf16[768,384]{1,0:T(8,128)(2,1)} %wv_own_hbm.1), channel_id=1, source_target_pairs={{0,1},{1,0},{2,3},{3,2},{4,5},{5,4},{6,7},{7,6},{8,9},{9,8},{10,11... | collective-permute-start | bytes 1769480 | tf_op jit(solution)/shard_map/ppermute | solution.py:1047
  1.8 19.3 %collective-permute-start.6 = (bf16[384,768]{1,0:T(8,128)(2,1)}, bf16[384,768]{1,0:T(8,128)(2,1)S(1)}, u32[]{:S(2)}, u32[]{:S(2)}) collective-permute-start(bf16[384,768]{1,0:T(8,128)(2,1)} %wo_own_hbm.1), channel_id=1, source_target_pairs={{0,1},{1,0},{2,3},{3,2},{4,5},{5,4},{6,7},{7,6},{8,9},{9,8},{10,11... | collective-permute-start | bytes 1769480 | tf_op jit(solution)/shard_map/ppermute | solution.py:1047
  3.0 17.9 %copy-start.4 = (bf16[6,32]{1,0:T(8,128)(2,1)}, bf16[6,32]{1,0:T(8,128)(2,1)S(1)}, u32[]{:S(2)}) copy-start(bf16[6,32]{1,0:T(8,128)(2,1)S(1)} %collective-permute-done.5.tab_ref) | copy-start | bytes 1156
  3.0 40.1 %collective-permute-start = (bf16[768,1536]{1,0:T(8,128)(2,1)}, bf16[768,1536]{1,0:T(8,128)(2,1)}, u32[]{:S(2)}, u32[]{:S(2)}) collective-permute-start(bf16[768,1536]{1,0:T(8,128)(2,1)} %win_own.1), channel_id=1, source_target_pairs={{0,1},{1,0},{2,3},{3,2},{4,5},{5,4},{6,7},{7,6},{8,9},{9,8},{10,11... | collective-permute-start | bytes 7077896 | tf_op jit(solution)/shard_map/ppermute | solution.py:1047
  3.4 17.6 %copy-start = (bf16[768,384]{1,0:T(8,128)(2,1)}, bf16[768,384]{1,0:T(8,128)(2,1)S(1)}, u32[]{:S(2)}) copy-start(bf16[768,384]{1,0:T(8,128)(2,1)S(1)} %collective-permute-done.2.wq.wq_oth_hbm) | copy-start | bytes 1769476
  3.4 39.7 %collective-permute-start.1 = (bf16[1536,768]{1,0:T(8,128)(2,1)}, bf16[1536,768]{1,0:T(8,128)(2,1)}, u32[]{:S(2)}, u32[]{:S(2)}) collective-permute-start(bf16[1536,768]{1,0:T(8,128)(2,1)} %wout_own.1), channel_id=1, source_target_pairs={{0,1},{1,0},{2,3},{3,2},{4,5},{5,4},{6,7},{7,6},{8,9},{9,8},{10,11... | collective-permute-start | bytes 7077896 | tf_op jit(solution)/shard_map/ppermute | solution.py:1047
  21.0 0.8 copy-start.1
  21.0 1.0 copy-start.2
  21.0 1.2 copy-start.3
